TPU v7x, 32 devices: a whole 2x2x4 slice. The times are simulated.
32 devices in a mesh: store: 4 (over z), scorer: 8 (over y, x, core).
Axes of the slice: x: 2, y: 2, z: 4, core: 2. Of those that a mesh axis runs over, the one named last changes fastest.
Arguments:
- store_rows: bfloat16 [65536, 256], P(('store', 'scorer')), may hold values from -11 to 11
- cluster_logsize: bfloat16 [65536], P(('store', 'scorer')), may hold values from 0 to 318
- cluster_home: int32 [65536], replicated, may hold values from 0 to 65535, as said below
- cluster_ids: int32 [256, 512], P(('store', 'scorer')), may hold values from 0 to 65535, as said below
- valid_count: int32 [256], P(('store', 'scorer')), may hold values from 64 to 512
- candidates: bfloat16 [256, 512, 256], P(('store', 'scorer')), may hold values from -11 to 11
- cand_count: int32 [256], P(('store', 'scorer')), may hold values from 0 to 512, as said below
- candidate_row: int32 [256, 512], P(('store', 'scorer')), may hold values from 0 to 16383, as said below
- query_proj: bfloat16 [256, 256], replicated, may hold values from -0.375 to 0.375
- key_proj: bfloat16 [256, 256], replicated, may hold values from -0.375 to 0.375
- value_proj: bfloat16 [256, 256], replicated, may hold values from -0.375 to 0.375
- out_proj: bfloat16 [256, 256], replicated, may hold values from -0.375 to 0.375
- mlp_first: bfloat16 [512, 512], replicated, may hold values from -0.25 to 0.25
- bias_first: float32 [512], replicated, may hold values from -3 to 3
- mlp_second: bfloat16 [512, 256], replicated, may hold values from -0.25 to 0.25
- bias_second: float32 [256], replicated, may hold values from -3 to 3
- score_proj: bfloat16 [256], replicated, may hold values from -0.375 to 0.375
Outputs:
- span_scores: float32 [65536], P(('store', 'scorer'))
Inputs may be any that keep to these rules, and one draw needn't show every extreme that they name: A permutation: cluster c is row cluster_home[c] of store_rows. `cluster_ids`: of the 4096 entries of one device's requests, exactly 128 name clusters whose rows lie on each device's rows of store_rows, valid slots or not. `cand_count`: the counts of the 8 devices of one store group sum to 16384; in every group one device has all its requests full. `candidate_row`: the valid candidates of a store group fill each of its 16384 rows once; rows c * 2048 to (c + 1) * 2048 - 1 form span c, held by the group's device of scorer index c. One device has at most 512 valid candidates in one span, and in every group one device has exactly 512 in each span. Padded slots hold 0.
All inputs are finite; a program needn't handle non-finite values.
Results may differ from a plain program's by a relative error of at most 0.0065.
Values may be sent and summed in bfloat16 or wider, within the bound.
No kernel may reach another device: no remote copies, remote signals or barrier semaphores. Data moves between devices by JAX's collectives and lax.ppermute only.
A program may use at most 128 MiB of HBM per device.

v0:
```python
import functools
import math

import jax
import jax.numpy as jnp
from jax import lax
from jax.experimental import pallas as pl
from jax.experimental.pallas import tpu as pltpu
from jax.sharding import PartitionSpec as P

HEADS = 4
LANES = 128
BLOCK = 16
DEAD = -1e30
HIGH = 65536
OFFSET_PIECES = 3
ROWS_AT_ONCE = 64
SUM_LEAST = 2.0**-100
SUM_MOST = 2.0**100
VMEM_LIMIT = 40 * 1024 * 1024


def dot(a, b):
    return jnp.dot(a, b, preferred_element_type=jnp.float32)


def dot_nt(a, b):
    return lax.dot_general(a, b, (((1,), (1,)), ((), ())), preferred_element_type=jnp.float32)


def hot(mask):
    return jnp.where(mask, 1.0, 0.0).astype(jnp.bfloat16)


def iota(shape, axis):
    return lax.broadcasted_iota(jnp.int32, shape, axis)


def whole(memory_space=pltpu.VMEM):
    return pl.BlockSpec(memory_space=memory_space)


def look_up(table_t, index, pieces):
    highs = table_t.shape[1]
    count = index.shape[1]
    rows = dot(table_t, hot(iota((highs, count), 0) == (index >> 7)))
    mine = iota((LANES, count), 0) == (index & (LANES - 1))
    found = jnp.zeros((1, count), jnp.float32)
    for piece in range(pieces):
        part = rows[piece * LANES : (piece + 1) * LANES]
        found = found + float(256**piece) * jnp.sum(
            jnp.where(mine, part, 0.0), axis=0, keepdims=True
        )
    return found


def ask_kernel(
    valid_ref, count_ref, ids_ref, home_ref, asked_ref, rank_ref, span_ref, table_ref, *, rows_dev
):
    requests, slots = ids_ref.shape
    devices, per_pair = asked_ref.shape
    pieces = table_ref.shape[0] // LANES
    for piece in range(pieces):
        part = (home_ref[...] >> (8 * piece)) & 255
        table_ref[piece * LANES : (piece + 1) * LANES, :] = jnp.transpose(
            part.astype(jnp.float32)
        ).astype(jnp.bfloat16)
    table = table_ref[...]
    upto = hot(iota((slots, slots), 0) <= iota((slots, slots), 1))
    carry = jnp.zeros((devices, 1), jnp.float32)
    asked = jnp.zeros((devices, 2 * per_pair), jnp.float32)
    for r in range(requests):
        row = look_up(table, ids_ref[r : r + 1, :], pieces).astype(jnp.int32)
        dev = row // rows_dev
        local = row - dev * rows_dev
        live = iota((1, slots), 1) < jnp.where(count_ref[r] > 0, valid_ref[r], 0)
        dest = jnp.where((iota((devices, slots), 0) == dev) & live, 1.0, 0.0)
        running = dot(dest.astype(jnp.bfloat16), upto) + carry
        carry = running[:, slots - 1 : slots]
        rank_f = jnp.sum(dest * running, axis=0, keepdims=True) - 1.0
        rank = rank_f.astype(jnp.int32)
        at_rank = iota((per_pair, slots), 0) == rank
        local_f = local.astype(jnp.float32)
        high_f = (local >> 8).astype(jnp.float32)
        low_f = local_f - 256.0 * high_f
        values = jnp.concatenate(
            [jnp.where(at_rank, low_f, 0.0), jnp.where(at_rank, high_f, 0.0)], axis=0
        )
        asked = asked + dot_nt(dest.astype(jnp.bfloat16), values.astype(jnp.bfloat16))
        rank_ref[r : r + 1, :] = jnp.where(live, dev * LANES + rank, -1)
        span_ref[r] = jnp.min(jnp.where(live, rank_f, 1e9)).astype(jnp.int32)
        span_ref[requests + r] = jnp.max(rank_f).astype(jnp.int32)
    most = jnp.max(carry, axis=0, keepdims=True)
    asked = asked[:, :per_pair] + 256.0 * asked[:, per_pair:] + HIGH * most
    asked_ref[...] = asked.astype(jnp.int32)


def ask(valid_count, cand_count, cluster_ids, home_table, devices, per_pair, rows_dev):
    requests, slots = cluster_ids.shape
    highs = home_table.shape[0]
    pieces = -(-(highs * LANES - 1).bit_length() // 8)
    return pl.pallas_call(
        functools.partial(ask_kernel, rows_dev=rows_dev),
        in_specs=[whole(pltpu.SMEM), whole(pltpu.SMEM), whole(), whole()],
        out_specs=[whole(), whole(), whole(pltpu.SMEM)],
        out_shape=[
            jax.ShapeDtypeStruct((devices, per_pair), jnp.int32),
            jax.ShapeDtypeStruct((requests, slots), jnp.int32),
            jax.ShapeDtypeStruct((2 * requests,), jnp.int32),
        ],
        scratch_shapes=[pltpu.VMEM((pieces * LANES, highs), jnp.bfloat16)],
        compiler_params=pltpu.CompilerParams(vmem_limit_bytes=VMEM_LIMIT),
        cost_estimate=pl.CostEstimate(
            flops=4_000_000_000, bytes_accessed=1_000_000, transcendentals=0
        ),
        name="ask",
    )(valid_count, cand_count, cluster_ids, home_table)


def serve_kernel(asked_ref, store_ref, size_ref, after_ref, *refs, first, sized):
    del after_ref
    *out_refs, most_ref, column_ref = refs
    devices, per_pair = asked_ref.shape
    rows_dev, width = store_ref.shape
    places = max(out_ref.shape[1] for out_ref in out_refs)
    most_ref[0] = jnp.max((asked_ref[...] // HIGH).astype(jnp.float32)).astype(jnp.int32)
    asked = asked_ref[...] & (HIGH - 1)
    column_ref[...] = jnp.zeros(column_ref.shape, jnp.int32)
    column_ref[1 : per_pair + 1, :] = jnp.transpose(asked.astype(jnp.float32)).astype(jnp.int32)
    group = math.gcd(devices, 1 << (384 // places).bit_length() - 1)
    store = store_ref[...]
    lanes = iota((places, rows_dev), 1)
    if sized:
        size_t = jnp.transpose(size_ref[...].astype(jnp.float32)).astype(jnp.bfloat16)
    for start in range(0, devices, group):
        picks = []
        for d in range(start, start + group):
            column = column_ref[first : first + places, d : d + 1]
            picks.append(hot(column == lanes))
        found = dot(jnp.concatenate(picks, axis=0), store).reshape(group, places, width)
        if sized:
            asked_of = [asked[d : d + 1, :] for d in range(start, start + group)]
            sizes = look_up(size_t, jnp.concatenate(asked_of, axis=1), 1)
            rest = jnp.zeros((1, width - per_pair), jnp.float32)
            for g in range(group):
                mine = sizes[:, g * per_pair : (g + 1) * per_pair]
                mine = jnp.concatenate([mine, rest], axis=1)
                top = jnp.where(iota((places, width), 0) == 0, mine, found[g])
                out_refs[0][start + g] = top.astype(jnp.bfloat16)
        else:
            found = found.astype(jnp.bfloat16)
            for out_ref in out_refs:
                out_ref[start : start + group] = found[:, : out_ref.shape[1], :]


def serve(asked_here, store_rows, size_table, after, first, place_counts, sized):
    devices, per_pair = asked_here.shape
    rows_dev, width = store_rows.shape
    places = max(place_counts)
    column_rows = max(first + places, -(-(per_pair + 1) // BLOCK) * BLOCK)
    return pl.pallas_call(
        functools.partial(serve_kernel, first=first, sized=sized),
        in_specs=[whole(), whole(), whole(), whole(pl.ANY)],
        out_specs=[whole() for _ in place_counts] + [whole(pltpu.SMEM)],
        out_shape=[
            jax.ShapeDtypeStruct((devices, count, width), jnp.bfloat16) for count in place_counts
        ]
        + [jax.ShapeDtypeStruct((1,), jnp.int32)],
        scratch_shapes=[pltpu.VMEM((column_rows, devices), jnp.int32)],
        compiler_params=pltpu.CompilerParams(vmem_limit_bytes=VMEM_LIMIT),
        cost_estimate=pl.CostEstimate(
            flops=2 * devices * places * rows_dev * width,
            bytes_accessed=2 * (rows_dev + devices * sum(place_counts)) * width,
            transcendentals=0,
        ),
        name="serve",
    )(asked_here, store_rows, size_table, after)


def column_of(row):
    return jnp.transpose(jnp.broadcast_to(row, (LANES, row.shape[1])))


def row_of(ref, r, columns):
    part = ref[:, columns]
    mine = jnp.where(iota(part.shape, 0) == r, part.astype(jnp.float32), 0.0)
    return jnp.sum(mine, axis=0, keepdims=True).astype(jnp.int32)


def prep_kernel(
    cand_ref, query_ref, first_ref, bias_first_ref, score_ref, rank_ref, after_ref, *out_refs
):
    queries_ref, base_ref, place_ref, score_cols_ref = out_refs
    devices = after_ref.shape[0]
    cands, width = cand_ref.shape[1:]
    size = width // HEADS
    lane = iota((cands, LANES), 1)
    score = jnp.broadcast_to(score_ref[...].astype(jnp.float32), (LANES, score_ref.shape[1]))
    score_cols_ref[...] = jnp.transpose(score).astype(jnp.bfloat16)

    def one_request(r, carry):
        queries = dot(cand_ref[r], query_ref[...])
        for h in range(HEADS):
            pair = queries[:, h // 2 * LANES : (h // 2 + 1) * LANES]
            own = lane // size == h % 2
            picks = jnp.where(lane % size < OFFSET_PIECES, 1.0, 0.0)
            queries_ref[r, h] = jnp.where(own, pair, picks).astype(jnp.bfloat16)
        base_ref[r] = dot(cand_ref[r], first_ref[:width, :]) + bias_first_ref[...]
        spot = row_of(rank_ref, r, slice(None))
        at = (spot & (LANES - 1)) + 1
        place = (at // BLOCK) * (devices * BLOCK) + (spot // LANES) * BLOCK + at % BLOCK
        place_ref[r] = column_of(jnp.where(spot >= 0, place, -1))
        return carry

    lax.fori_loop(0, cand_ref.shape[0], one_request, 0)


def prep(candidates, query_proj, mlp_first, bias_first, score_proj, ranks, after):
    requests, cands, width = candidates.shape
    units = mlp_first.shape[1]
    return pl.pallas_call(
        prep_kernel,
        in_specs=[whole() for _ in range(6)] + [whole(pl.ANY)],
        out_specs=[whole() for _ in range(4)],
        out_shape=[
            jax.ShapeDtypeStruct((requests, HEADS, cands, LANES), jnp.bfloat16),
            jax.ShapeDtypeStruct((requests, cands, units), jnp.float32),
            jax.ShapeDtypeStruct((*ranks.shape, LANES), jnp.int32),
            jax.ShapeDtypeStruct((score_proj.shape[1], LANES), jnp.bfloat16),
        ],
        compiler_params=pltpu.CompilerParams(vmem_limit_bytes=VMEM_LIMIT),
        cost_estimate=pl.CostEstimate(
            flops=2 * requests * cands * width * (width + units),
            bytes_accessed=18 * requests * cands * width,
            transcendentals=0,
        ),
        name="prep",
    )(candidates, query_proj, mlp_first, bias_first, score_proj, ranks, after)


def score_kernel(*refs, bases, from_place, to_place, spare):
    valid_ref, count_ref, span_ref, before_flag_ref = refs[:4]
    base_all, queries_all, place_all, rank_ref, target_ref = refs[4:9]
    arrived_all = refs[9 : 9 + len(bases)]
    (
        key_ref,
        value_ref,
        out_proj_ref,
        first_ref,
        second_ref,
        bias_second_ref,
        score_ref,
        before_ref,
        table_ref,
        flag_ref,
        rows_ref,
        keys_ref,
        values_ref,
        context_ref,
        least_ref,
        most_ref,
        size_ref,
        base_ref,
        queries_ref,
        place_ref,
        arrived_sems,
        request_sems,
        *arrived_refs,
    ) = refs[9 + len(bases) :]
    requests, slots = rank_ref.shape
    devices = arrived_refs[0].shape[0]
    cands = base_ref.shape[1]
    width = rows_ref.shape[1]
    head_size = width // HEADS
    cand_part = math.gcd(cands, 256)
    highs = table_ref.shape[0]
    scale = math.sqrt(head_size)
    to_log2 = math.log2(math.e) / scale
    sizes_done = range(slots // 2, slots + 1, LANES)
    at_hand = len(bases) - 1 if spare else len(bases)
    fetched = ((place_all, place_ref), (queries_all, queries_ref), (base_all, base_ref))
    own_rows = [slice(h % 2 * head_size, (h % 2 + 1) * head_size) for h in range(HEADS)]
    other_rows = [slice((1 - h % 2) * head_size, (2 - h % 2) * head_size) for h in range(HEADS)]

    def is_mine(r):
        last_place = span_ref[requests + r] + 1
        return (count_ref[r] > 0) & (last_place >= from_place) & (last_place < to_place)

    def copies_of(r):
        return [
            pltpu.make_async_copy(source.at[r], target.at[r], request_sems.at[i, r])
            for i, (source, target) in enumerate(fetched)
        ]

    arrivals = [
        pltpu.make_async_copy(source, target, arrived_sems.at[i])
        for i, (source, target) in enumerate(zip(arrived_all, arrived_refs))
    ]
    for copy in arrivals[:at_hand]:
        copy.start()
    for r in range(requests):

        @pl.when(is_mine(r))
        def _():
            for copy in copies_of(r):
                copy.start()

    keys_ref[...] = jnp.zeros(keys_ref.shape, jnp.bfloat16)
    values_ref[...] = jnp.zeros(values_ref.shape, jnp.bfloat16)
    for copy in arrivals[:at_hand]:
        copy.wait()
    heads_of = arrived_refs[0][:, :BLOCK, :LANES].astype(jnp.float32)
    at_top = iota(heads_of.shape, 1) == 0
    sizes = jnp.sum(jnp.where(at_top, heads_of, 0.0), axis=1)
    size_ref[...] = jnp.transpose(sizes).astype(jnp.bfloat16)

    def select(r, n, arrived_ref, base):
        block_rows = devices * BLOCK
        blocks = arrived_ref.shape[1] // BLOCK
        at_once = min(2, blocks)
        low_block = jnp.clip((span_ref[r] + 1) // BLOCK - base, 0, blocks)
        high_block = jnp.clip((span_ref[requests + r] + 1) // BLOCK + 1 - base, 0, blocks)

        def step(i, carry):
            wanted = low_block + i * at_once
            j = jnp.minimum(wanted, blocks - at_once)
            place = place_ref[r, :n, :]
            rel = jnp.where(place >= (wanted + base) * block_rows, place, -1)
            rel = rel - (j + base) * block_rows
            lanes = iota((n, LANES), 1)
            found = []
            for b in range(at_once):
                start = pl.multiple_of((j + b) * BLOCK, BLOCK)
                block = arrived_ref[:, pl.ds(start, BLOCK), :].reshape(block_rows, width)
                firsts = range(b * block_rows, (b + 1) * block_rows, LANES)
                picks = [hot(rel == lanes + first) for first in firsts]
                found.append(dot(jnp.concatenate(picks, axis=1), block))
            rows_ref[:n, :] += sum(found)
            return carry

        lax.fori_loop(0, (high_block - low_block + at_once - 1) // at_once, step, 0)

    def load(r, n, blocks_at_hand):
        rows_ref[:n, :] = jnp.zeros((n, width), jnp.float32)
        for arrived_ref, base in list(zip(arrived_refs, bases))[:blocks_at_hand]:
            select(r, n, arrived_ref, base)
        spot = row_of(rank_ref, r, slice(0, n))
        size = look_up(size_ref[...], spot, 1)
        largest = jnp.max(jnp.where(spot >= 0, size, DEAD), axis=1, keepdims=True)
        left = jnp.where(spot >= 0, (size - largest) * scale, DEAD)
        pieces = jnp.zeros((head_size, n), jnp.float32)
        for row in range(OFFSET_PIECES):
            piece = left.astype(jnp.bfloat16).astype(jnp.float32)
            left = left - piece
            pieces = jnp.where(iota((head_size, n), 0) == row, piece, pieces)
        pieces = pieces.astype(jnp.bfloat16)
        rows = rows_ref[:n, :].astype(jnp.bfloat16)
        keys = dot_nt(key_ref[...], rows).astype(jnp.bfloat16)
        values = dot(rows, value_ref[...])
        own = iota((n, LANES), 1) // head_size
        for h in range(HEADS):
            keys_ref[h, own_rows[h], :n] = keys[h * head_size : (h + 1) * head_size]
            keys_ref[h, other_rows[h], :n] = pieces
            if n < slots:
                rest = (head_size, slots - n)
                dead = jnp.where(iota(rest, 0) == 0, DEAD, 0.0).astype(jnp.bfloat16)
                keys_ref[h, other_rows[h], n:] = dead
            pair = values[:, h // 2 * LANES : (h // 2 + 1) * LANES]
            first = h % 2 * n
            values_ref[h // 2, first : first + n, :] = jnp.where(own == h % 2, pair, 0.0).astype(
                jnp.bfloat16
            )

    def attend(r, n, slot):
        least = least_ref[...]
        most = most_ref[...]
        for pair in range(HEADS // 2):
            probs = []
            for h in (2 * pair, 2 * pair + 1):
                logits = dot(queries_ref[r, h], keys_ref[h, :, :n])
                of_head = []
                for first in range(0, cands, ROWS_AT_ONCE):
                    weights = jnp.exp2(logits[first : first + ROWS_AT_ONCE] * to_log2)
                    total = jnp.sum(weights, axis=1, keepdims=True)
                    least = jnp.minimum(least, total)
                    most = jnp.maximum(most, total)
                    of_head.append((weights * (1.0 / total)).astype(jnp.bfloat16))
                probs.append(jnp.concatenate(of_head, axis=0))
            context = dot(jnp.concatenate(probs, axis=1), values_ref[pair, : 2 * n, :])
            context_ref[slot, :, pair * LANES : (pair + 1) * LANES] = context.astype(jnp.bfloat16)
        least_ref[...] = least
        most_ref[...] = most

    def attend_exactly(r, slot):
        def part(c, carry):
            rows = pl.ds(pl.multiple_of(c * cand_part, cand_part), cand_part)
            for pair in range(HEADS // 2):
                probs = []
                for h in (2 * pair, 2 * pair + 1):
                    logits = dot(queries_ref[r, h, rows, :], keys_ref[h])
                    top = jnp.max(logits, axis=1, keepdims=True)
                    weights = jnp.exp2((logits - top) * to_log2)
                    total = jnp.sum(weights, axis=1, keepdims=True)
                    probs.append((weights * (1.0 / total)).astype(jnp.bfloat16))
                context = dot(jnp.concatenate(probs, axis=1), values_ref[pair])
                columns = slice(pair * LANES, (pair + 1) * LANES)
                context_ref[slot, rows, columns] = context.astype(jnp.bfloat16)
            return carry

        lax.fori_loop(0, cands // cand_part, part, 0)

    def rate(last, slot):
        r = jnp.maximum(last, 0)
        attended = dot(context_ref[slot], out_proj_ref[...]).astype(jnp.bfloat16)
        hidden = dot(attended, first_ref[width:, :]) + base_ref[r]
        hidden = jnp.maximum(hidden, 0.0).astype(jnp.bfloat16)
        hidden = dot(hidden, second_ref[...]) + bias_second_ref[...]
        hidden = jnp.maximum(hidden, 0.0).astype(jnp.bfloat16)
        scores = jnp.transpose(dot(hidden, score_ref[...]))[:1]
        target = row_of(target_ref, r, slice(None))
        counted = iota((1, cands), 1) < jnp.where(last >= 0, count_ref[r], 0)
        high_hot = hot((iota((highs, cands), 0) == (target >> 7)) & counted)
        at_low = iota((LANES, cands), 0) == (target & (LANES - 1))
        left = jnp.where(counted, scores, 0.0)
        pieces = []
        for _ in range(3):
            piece = left.astype(jnp.bfloat16).astype(jnp.float32)
            left = left - piece
            pieces.append(jnp.where(at_low, piece, 0.0).astype(jnp.bfloat16))
        found = dot_nt(high_hot, jnp.concatenate(pieces, axis=0))
        table_ref[...] += sum(found[:, i * LANES : (i + 1) * LANES] for i in range(3))

    def one_request(r, carry):
        last, slot = carry
        valid = valid_ref[r]
        mine = is_mine(r)

        @pl.when(mine)
        def _():
            for copy in copies_of(r):
                copy.wait()
            fewer = 0
            for n in sizes_done:

                @pl.when((valid > fewer) & (valid <= n))
                def _():
                    load(r, n, at_hand)
                    rate(last, slot)
                    attend(r, n, 1 - slot)

                fewer = n

        return jnp.where(mine, r, last), jnp.where(mine, 1 - slot, slot)

    table_ref[...] = before_ref[...]
    least_ref[...] = jnp.ones(least_ref.shape, jnp.float32)
    most_ref[...] = jnp.ones(most_ref.shape, jnp.float32)
    context_ref[...] = jnp.zeros(context_ref.shape, jnp.bfloat16)
    last, slot = lax.fori_loop(0, requests, one_request, (jnp.int32(-1), jnp.int32(0)))

    @pl.when(last >= 0)
    def _():
        rate(last, slot)

    in_range = (jnp.min(least_ref[...]) >= SUM_LEAST) & (jnp.max(most_ref[...]) <= SUM_MOST)
    again = jnp.logical_not(in_range) | (before_flag_ref[0] > 0)
    flag_ref[0] = again.astype(jnp.int32)
    if not spare:
        return
    for r in range(requests):
        again = again | ((count_ref[r] > 0) & (span_ref[requests + r] + 1 >= to_place))

    def exactly(r, carry):
        @pl.when(count_ref[r] > 0)
        def _():
            for copy in copies_of(r):
                copy.start()
            for copy in copies_of(r):
                copy.wait()
            load(r, slots, len(bases))
            attend_exactly(r, 0)
            rate(r, 0)

        return carry

    @pl.when(again)
    def _():
        arrivals[-1].start()
        arrivals[-1].wait()
        table_ref[...] = jnp.zeros(table_ref.shape, jnp.float32)
        lax.fori_loop(0, requests, exactly, 0)


def score(scalars, operands, arrived, weights, before, places, spare=False):
    base, queries, columns, ranks, _ = operands
    cands, width = base.shape[1], arrived[0].shape[2]
    slots = ranks.shape[1]
    devices = arrived[0].shape[0]
    bases = []
    for rows in arrived:
        bases.append(bases[-1] + arrived[len(bases) - 1].shape[1] // BLOCK if bases else 0)
    operands = [*operands, *arrived, *weights, before]
    return pl.pallas_call(
        functools.partial(
            score_kernel,
            bases=tuple(bases),
            from_place=places[0],
            to_place=places[1],
            spare=spare,
        ),
        in_specs=[whole(pltpu.SMEM)] * 4
        + [whole(pl.ANY)] * 3
        + [whole()] * 2
        + [whole(pl.ANY)] * len(arrived)
        + [whole() for _ in (*weights, before)],
        out_specs=[whole(), whole(pltpu.SMEM)],
        scratch_shapes=[
            pltpu.VMEM((slots, width), jnp.float32),
            pltpu.VMEM((HEADS, LANES, slots), jnp.bfloat16),
            pltpu.VMEM((HEADS // 2, 2 * slots, LANES), jnp.bfloat16),
            pltpu.VMEM((2, cands, width), jnp.bfloat16),
            pltpu.VMEM((ROWS_AT_ONCE, 1), jnp.float32),
            pltpu.VMEM((ROWS_AT_ONCE, 1), jnp.float32),
            pltpu.VMEM((LANES, devices), jnp.bfloat16),
            pltpu.VMEM(base.shape, base.dtype),
            pltpu.VMEM(queries.shape, queries.dtype),
            pltpu.VMEM(columns.shape, columns.dtype),
            pltpu.SemaphoreType.DMA((len(arrived),)),
            pltpu.SemaphoreType.DMA((3, ranks.shape[0])),
            *(pltpu.VMEM(rows.shape, rows.dtype) for rows in arrived),
        ],
        out_shape=[
            jax.ShapeDtypeStruct(before.shape, jnp.float32),
            jax.ShapeDtypeStruct((1,), jnp.int32),
        ],
        compiler_params=pltpu.CompilerParams(vmem_limit_bytes=VMEM_LIMIT),
        cost_estimate=pl.CostEstimate(
            flops=10_000_000_000, bytes_accessed=5_000_000, transcendentals=4_000_000
        ),
        name="score",
    )(*scalars, *operands)


def on_device(
    store_rows,
    cluster_logsize,
    cluster_home,
    cluster_ids,
    valid_count,
    candidates,
    cand_count,
    candidate_row,
    query_proj,
    key_proj,
    value_proj,
    out_proj,
    mlp_first,
    bias_first,
    mlp_second,
    bias_second,
    score_proj,
):
    axes = ("store", "scorer")
    devices = lax.axis_size(axes)
    scorers = lax.axis_size("scorer")
    requests, slots = cluster_ids.shape
    rows_dev, width = store_rows.shape
    cands = candidates.shape[1]
    per_pair = requests * slots // devices
    span_live = requests * cands // 2

    exchange = functools.partial(
        lax.all_to_all, axis_name=axes, split_axis=0, concat_axis=0, tiled=True
    )
    asked, ranks, span = ask(
        valid_count,
        cand_count,
        cluster_ids,
        cluster_home.reshape(-1, LANES),
        devices,
        per_pair,
        rows_dev,
    )
    asked_here = exchange(asked)
    in_blocks = lambda places: -(-places // BLOCK) * BLOCK
    early = in_blocks(per_pair // 2)
    cuts = (0, early, in_blocks(7 * per_pair // 8), in_blocks(per_pair + 1))
    lookup = (asked_here, store_rows, cluster_logsize.reshape(-1, LANES))
    early_here, most = serve(*lookup, asked_here, 0, [early], True)
    early_rows = exchange(early_here)
    queries, base, columns, score_cols = prep(
        candidates,
        query_proj,
        mlp_first,
        bias_first.reshape(1, -1),
        score_proj.reshape(1, -1),
        ranks,
        early_here,
    )
    last_rows = lax.cond(
        most[0] + 1 > cuts[2],
        lambda: exchange(serve(*lookup, score_cols, cuts[2], [cuts[3] - cuts[2]], False)[0]),
        lambda: jnp.zeros((devices, cuts[3] - cuts[2], width), jnp.bfloat16),
    )
    late_here, _ = serve(*lookup, last_rows, cuts[1], [cuts[2] - cuts[1]], False)
    weights = (
        key_proj.T,
        value_proj,
        out_proj,
        mlp_first,
        mlp_second,
        bias_second.reshape(1, -1),
        score_cols,
    )
    table = jnp.zeros((scorers * span_live // LANES, LANES), jnp.float32)
    scalars = (valid_count, cand_count, span)
    shared = (base, queries, columns, ranks, candidate_row)
    late_here, early_rows = lax.optimization_barrier((late_here, early_rows))
    late_rows = exchange(late_here)
    no_flag = jnp.zeros((1,), jnp.int32)
    arrived = (early_rows,)
    table, flag = score((*scalars, no_flag), shared, arrived, weights, table, cuts[0:2])
    arrived = (early_rows, late_rows, last_rows)
    table, _ = score((*scalars, flag), shared, arrived, weights, table, cuts[1:3], spare=True)
    parts = lax.all_to_all(
        table.reshape(scorers, span_live // LANES, LANES),
        "scorer",
        split_axis=0,
        concat_axis=0,
        tiled=True,
    )
    return jnp.sum(parts, axis=0).reshape(span_live)


def solution(mesh):
    rows = P(("store", "scorer"))
    in_specs = (
        P(("store", "scorer"), None),
        rows,
        P(),
        P(("store", "scorer"), None),
        rows,
        P(("store", "scorer"), None, None),
        rows,
        P(("store", "scorer"), None),
    ) + (P(),) * 9
    return jax.shard_map(
        on_device, mesh=mesh, in_specs=in_specs, out_specs=rows, check_vma=False
    )
```

profile of v0, /device:TPU:0, one launch (start us, length us, event | category | flops | bytes accessed | tf_op | source)
XLA Modules:
  0.0 119.9 jit_solution(18077160184073214217)
XLA Ops:
  0.0 0.9 copy-done.2
  1.0 0.7 copy-done.7
  1.7 0.7 copy-done.11
  2.3 0.7 copy-done.13
  3.0 5.2 %ask.1 = (s32[32,128]{1,0:T(8,128)}, s32[8,512]{1,0:T(8,128)S(1)}, s32[16]{0:T(128)S(1)}) custom-call(s32[8]{0:T(128)S(1)} %copy-done.11, s32[8]{0:T(128)S(1)} %copy-done.13, s32[8,512]{1,0:T(8,128)S(1)} %copy-done.7, s32[512,128]{1,0:T(8,128)S(1)} %bitcast.15), custom_call_target="tpu_custom_call" | custom-call | flops 4000000000 | bytes 1000000 | tf_op jit(solution)/shard_map/ask/pallas_call | solution.py:102
  8.2 0.0 copy-start
  8.2 0.0 copy-start.1
  8.2 0.0 copy-start.4
  8.2 0.0 copy-start.9
  8.2 7.3 %all-to-all-start.1 = ((s32[32,1,128]{2,1,0:T(1,128)}), s32[32,1,128]{2,1,0:T(1,128)S(1)}, u32[]{:S(2)}, u32[]{:S(2)}) async-start(s32[32,1,128]{2,1,0:T(1,128)} %bitcast.3), calls=%async_computation.1 | async-start | bytes 32768 | tf_op jit(solution)/shard_map/all_to_all | solution.py:584
  15.6 0.0 copy-done.24
  15.6 7.1 %all-to-all-done.1 = s32[32,1,128]{2,1,0:T(1,128)S(1)} async-done(((s32[32,1,128]{2,1,0:T(1,128)}), s32[32,1,128]{2,1,0:T(1,128)S(1)}, u32[]{:S(2)}, u32[]{:S(2)}) %all-to-all-start.1) | async-done | bytes 16416 | tf_op jit(solution)/shard_map/all_to_all | solution.py:584
  22.7 0.0 copy-done.23
  22.7 4.9 %serve.4 = (bf16[32,64,256]{2,1,0:T(8,128)(2,1)}, s32[1]{0:T(128)}) custom-call(s32[32,128]{1,0:T(8,128)S(1)} %bitcast.19, bf16[2048,256]{1,0:T(8,128)(2,1)} %store_ref.3, bf16[16,128]{1,0:T(8,128)(2,1)S(1)} %bitcast.23, s32[32,128]{1,0:T(8,128)S(1)} %bitcast.20), custom_call_target="tpu_custom_call" | custom-call | flops 2147483648 | bytes 2097152 | tf_op jit(solution)/shard_map/serve/pallas_call | solution.py:161
  28.3 0.0 copy-done
  28.3 0.0 copy-done.1
  28.3 0.0 copy-done.4
  28.3 0.0 copy-done.9
  28.3 6.4 %prep.1 = (bf16[8,4,512,128]{3,2,1,0:T(8,128)(2,1)S(1)}, f32[8,512,512]{2,1,0:T(8,128)}, s32[8,512,128]{2,1,0:T(8,128)S(1)}, bf16[256,128]{1,0:T(8,128)(2,1)S(1)}) custom-call(bf16[8,512,256]{2,1,0:T(8,128)(2,1)S(1)} %copy-done, bf16[256,256]{1,0:T(8,128)(2,1)S(1)} %copy-done.4, bf16[512,512]{1,0:T(8,128)(2,1)S(1)} %copy-done.1, f32[1,512]{1,0:T(1,128)S(1)} %bitcast.16, ...), custom_call_target="tpu_custom_call" | custom-call | flops 1610612736 | bytes 18874368 | tf_op jit(solution)/shard_map/prep/pallas_call | solution.py:221
  34.7 2.0 %copy-done.15 = bf16[8,4,512,128]{3,2,1,0:T(8,128)(2,1)} copy-done((bf16[8,4,512,128]{3,2,1,0:T(8,128)(2,1)}, bf16[8,4,512,128]{3,2,1,0:T(8,128)(2,1)S(1)}, u32[]{:S(2)}) %copy-start.15) | copy-done | bytes 4194328
  36.7 1.3 %copy-done.18 = s32[8,512,128]{2,1,0:T(8,128)} copy-done((s32[8,512,128]{2,1,0:T(8,128)}, s32[8,512,128]{2,1,0:T(8,128)S(1)}, u32[]{:S(2)}) %copy-start.18) | copy-done | bytes 2097176
  38.0 0.1 conditional.1
  38.0 0.1 broadcast.2
  38.1 0.0 copy-start.21
  38.1 2.7 %all-to-all-start.2 = ((bf16[32,64,256]{2,1,0:T(8,128)(2,1)}), bf16[32,64,256]{2,1,0:T(8,128)(2,1)S(1)}, u32[]{:S(2)}, u32[]{:S(2)}) async-start(bf16[32,64,256]{2,1,0:T(8,128)(2,1)} %get-tuple-element.39.after_ref), calls=%async_computation.2 | async-start | bytes 2097152 | tf_op jit(solution)/shard_map/all_to_all | solution.py:590
  40.8 0.0 copy-start.22
  40.8 0.0 copy-start.3
  40.8 0.0 copy-start.5
  40.8 0.0 copy-start.6
  40.8 0.0 copy-start.8
  40.8 0.0 copy-start.10
  40.8 0.0 copy-start.12
  40.8 0.0 copy-start.14
  40.9 4.2 %serve.5 = (bf16[32,48,256]{2,1,0:T(8,128)(2,1)}, s32[1]{0:T(128)}) custom-call(s32[32,128]{1,0:T(8,128)S(1)} %bitcast.22, bf16[2048,256]{1,0:T(8,128)(2,1)} %store_ref.3, bf16[16,128]{1,0:T(8,128)(2,1)S(1)} %bitcast.25, bf16[32,32,256]{2,1,0:T(8,128)(2,1)S(1)} %get-tuple-element.51.after_ref.refs_11_), custom_call_target="tpu_custom_call" | custom-call | flops 1610612736 | bytes 1835008 | tf_op jit(solution)/shard_map/serve/pallas_call | solution.py:161
  45.1 21.9 %all-to-all-done.2.refs_9_ = bf16[32,64,256]{2,1,0:T(8,128)(2,1)S(1)} async-done(((bf16[32,64,256]{2,1,0:T(8,128)(2,1)}), bf16[32,64,256]{2,1,0:T(8,128)(2,1)S(1)}, u32[]{:S(2)}, u32[]{:S(2)}) %all-to-all-start.2) | async-done | bytes 1048608 | tf_op jit(solution)/shard_map/all_to_all | solution.py:590
  67.0 0.0 copy-done.21
  67.0 3.5 %all-to-all-start.3 = ((bf16[32,48,256]{2,1,0:T(8,128)(2,1)}), bf16[32,48,256]{2,1,0:T(8,128)(2,1)S(1)}, u32[]{:S(2)}, u32[]{:S(2)}) async-start(bf16[32,48,256]{2,1,0:T(8,128)(2,1)} %get-tuple-element.48), calls=%async_computation.3 | async-start | bytes 1572864 | tf_op jit(solution)/shard_map/all_to_all | solution.py:619
  70.5 0.0 copy-done.22
  70.5 0.1 copy.20
  70.7 2.2 %copy-done.16 = bf16[8,4,512,128]{3,2,1,0:T(8,128)(2,1)S(1)} copy-done((bf16[8,4,512,128]{3,2,1,0:T(8,128)(2,1)S(1)}, bf16[8,4,512,128]{3,2,1,0:T(8,128)(2,1)}, u32[]{:S(2)}) %copy-start.16) | copy-done | bytes 4194328
  72.9 1.6 %copy-done.19 = s32[8,512,128]{2,1,0:T(8,128)S(1)} copy-done((s32[8,512,128]{2,1,0:T(8,128)S(1)}, s32[8,512,128]{2,1,0:T(8,128)}, u32[]{:S(2)}) %copy-start.19) | copy-done | bytes 2097176
  74.5 9.0 %score.2 = (f32[128,128]{1,0:T(8,128)S(1)}, s32[1]{0:T(128)}) custom-call(s32[8]{0:T(128)S(1)} %copy-done.12, s32[8]{0:T(128)S(1)} %copy-done.14, s32[16]{0:T(128)S(1)} %get-tuple-element.36.refs_2_, s32[1]{0:T(128)} %constant.2.clone.1.refs_3_, f32[8,512,512]{2,1,0:T(8,128)} %get-tuple-element.40.refs_4_, bf16[8,4,512,128]{3,2,1,0:T(8,128)(2,1)S(1)} %copy-done.16, ...), custom_call_target="tpu_custom_call" | custom-call | flops 10000000000 | bytes 5000000 | tf_op jit(solution)/shard_map/score/pallas_call | solution.py:503
  83.5 7.6 %all-to-all-done.3.refs_10_ = bf16[32,48,256]{2,1,0:T(8,128)(2,1)S(1)} async-done(((bf16[32,48,256]{2,1,0:T(8,128)(2,1)}), bf16[32,48,256]{2,1,0:T(8,128)(2,1)S(1)}, u32[]{:S(2)}, u32[]{:S(2)}) %all-to-all-start.3) | async-done | bytes 786464 | tf_op jit(solution)/shard_map/all_to_all | solution.py:619
  91.1 2.2 %copy-done.17 = bf16[8,4,512,128]{3,2,1,0:T(8,128)(2,1)S(1)} copy-done((bf16[8,4,512,128]{3,2,1,0:T(8,128)(2,1)S(1)}, bf16[8,4,512,128]{3,2,1,0:T(8,128)(2,1)}, u32[]{:S(2)}) %copy-start.17) | copy-done | bytes 4194328
  93.3 1.6 %copy-done.20 = s32[8,512,128]{2,1,0:T(8,128)S(1)} copy-done((s32[8,512,128]{2,1,0:T(8,128)S(1)}, s32[8,512,128]{2,1,0:T(8,128)}, u32[]{:S(2)}) %copy-start.20) | copy-done | bytes 2097176
  94.9 3.2 %score.3 = (f32[128,128]{1,0:T(8,128)S(1)}, s32[1]{0:T(128)}) custom-call(s32[8]{0:T(128)S(1)} %copy-done.12, s32[8]{0:T(128)S(1)} %copy-done.14, s32[16]{0:T(128)S(1)} %get-tuple-element.36.refs_2_, s32[1]{0:T(128)} %get-tuple-element.47.refs_3_, f32[8,512,512]{2,1,0:T(8,128)} %get-tuple-element.40.refs_4_, bf16[8,4,512,128]{3,2,1,0:T(8,128)(2,1)S(1)} %copy-done.17, ...), custom_call_target="tpu_custom_call" | custom-call | flops 10000000000 | bytes 5000000 | tf_op jit(solution)/shard_map/score/pallas_call | solution.py:503
  98.1 21.2 %all_to_all.31 = f32[8,16,128]{2,1,0:T(8,128)S(1)} all-to-all(f32[8,16,128]{2,1,0:T(8,128)S(1)} %bitcast.14), channel_id=1, replica_groups=mesh['store'=4,'scorer'=8] {'scorer'}, dimensions={0} | all-to-all | bytes 131072 | tf_op jit(solution)/shard_map/all_to_all | solution.py:625
  119.3 0.6 reduce_sum.9
  (21 shorter events, 0.0 us)
Async XLA Ops:
  0.0 0.9 copy-start.2
  1.0 0.7 copy-start.7
  1.7 0.7 copy-start.11
  2.3 0.7 copy-start.13
  3.0 12.6 %copy-start.24 = (bf16[256]{0:T(256)(128)(2,1)S(1)}, bf16[256]{0:T(256)(128)(2,1)}, u32[]{:S(2)}) copy-start(bf16[256]{0:T(256)(128)(2,1)} %param.35) | copy-start | bytes 1540
  3.0 19.7 %copy-start.23 = (bf16[2048]{0:T(1024)(128)(2,1)S(1)}, bf16[2048]{0:T(1024)(128)(2,1)}, u32[]{:S(2)}) copy-start(bf16[2048]{0:T(1024)(128)(2,1)} %param.20) | copy-start | bytes 12292
  8.2 20.1 %copy-start = (bf16[8,512,256]{2,1,0:T(8,128)(2,1)S(1)}, bf16[8,512,256]{2,1,0:T(8,128)(2,1)}, u32[]{:S(2)}) copy-start(bf16[8,512,256]{2,1,0:T(8,128)(2,1)} %cand_ref.1) | copy-start | bytes 6291460
  8.2 20.1 %copy-start.1 = (bf16[512,512]{1,0:T(8,128)(2,1)S(1)}, bf16[512,512]{1,0:T(8,128)(2,1)}, u32[]{:S(2)}) copy-start(bf16[512,512]{1,0:T(8,128)(2,1)} %refs_15_.1) | copy-start | bytes 1572868
  8.2 20.1 %copy-start.4 = (bf16[256,256]{1,0:T(8,128)(2,1)S(1)}, bf16[256,256]{1,0:T(8,128)(2,1)}, u32[]{:S(2)}) copy-start(bf16[256,256]{1,0:T(8,128)(2,1)} %query_ref.1) | copy-start | bytes 393220
  8.2 20.1 %copy-start.9 = (f32[512]{0:T(512)S(1)}, f32[512]{0:T(512)}, u32[]{:S(2)}) copy-start(f32[512]{0:T(512)} %param.32) | copy-start | bytes 6148
  8.2 14.5 %all-to-all-start.1 = ((s32[32,1,128]{2,1,0:T(1,128)}), s32[32,1,128]{2,1,0:T(1,128)S(1)}, u32[]{:S(2)}, u32[]{:S(2)}) async-start(s32[32,1,128]{2,1,0:T(1,128)} %bitcast.3), calls=%async_computation.1 | async-start | bytes 32768 | tf_op jit(solution)/shard_map/all_to_all | solution.py:584
  34.7 2.0 %copy-start.15 = (bf16[8,4,512,128]{3,2,1,0:T(8,128)(2,1)}, bf16[8,4,512,128]{3,2,1,0:T(8,128)(2,1)S(1)}, u32[]{:S(2)}) copy-start(bf16[8,4,512,128]{3,2,1,0:T(8,128)(2,1)S(1)} %get-tuple-element.41.refs_5_) | copy-start | bytes 12582916
  36.7 1.3 %copy-start.18 = (s32[8,512,128]{2,1,0:T(8,128)}, s32[8,512,128]{2,1,0:T(8,128)S(1)}, u32[]{:S(2)}) copy-start(s32[8,512,128]{2,1,0:T(8,128)S(1)} %get-tuple-element.42.refs_6_) | copy-start | bytes 6291460
  38.1 28.9 %copy-start.21 = (bf16[32,32,256]{2,1,0:T(8,128)(2,1)}, bf16[32,32,256]{2,1,0:T(8,128)(2,1)S(1)}, u32[]{:S(2)}) copy-start(bf16[32,32,256]{2,1,0:T(8,128)(2,1)S(1)} %get-tuple-element.51.after_ref.refs_11_) | copy-start | bytes 1572868
  38.1 28.9 %all-to-all-start.2 = ((bf16[32,64,256]{2,1,0:T(8,128)(2,1)}), bf16[32,64,256]{2,1,0:T(8,128)(2,1)S(1)}, u32[]{:S(2)}, u32[]{:S(2)}) async-start(bf16[32,64,256]{2,1,0:T(8,128)(2,1)} %get-tuple-element.39.after_ref), calls=%async_computation.2 | async-start | bytes 2097152 | tf_op jit(solution)/shard_map/all_to_all | solution.py:590
  40.8 29.8 %copy-start.22 = (bf16[256,256]{1,0:T(8,128)(2,1)S(1)}, bf16[256,256]{1,0:T(8,128)(2,1)}, u32[]{:S(2)}) copy-start(bf16[256,256]{1,0:T(8,128)(2,1)} %param.28) | copy-start | bytes 393220
  40.8 29.9 %copy-start.3 = (bf16[512,256]{1,0:T(8,128)(2,1)S(1)}, bf16[512,256]{1,0:T(8,128)(2,1)}, u32[]{:S(2)}) copy-start(bf16[512,256]{1,0:T(8,128)(2,1)} %refs_16_.1) | copy-start | bytes 786436
  40.8 29.9 %copy-start.5 = (bf16[256,256]{1,0:T(8,128)(2,1)S(1)}, bf16[256,256]{1,0:T(8,128)(2,1)}, u32[]{:S(2)}) copy-start(bf16[256,256]{1,0:T(8,128)(2,1)} %refs_13_.3) | copy-start | bytes 393220
  40.8 29.9 %copy-start.6 = (bf16[256,256]{1,0:T(8,128)(2,1)S(1)}, bf16[256,256]{1,0:T(8,128)(2,1)}, u32[]{:S(2)}) copy-start(bf16[256,256]{1,0:T(8,128)(2,1)} %refs_14_.3) | copy-start | bytes 393220
  40.8 29.9 %copy-start.8 = (s32[8,512]{1,0:T(8,128)S(1)}, s32[8,512]{1,0:T(8,128)}, u32[]{:S(2)}) copy-start(s32[8,512]{1,0:T(8,128)} %refs_8_.3) | copy-start | bytes 49156
  40.8 29.9 %copy-start.10 = (f32[256]{0:T(256)S(1)}, f32[256]{0:T(256)}, u32[]{:S(2)}) copy-start(f32[256]{0:T(256)} %param.34) | copy-start | bytes 3076
  40.8 29.9 %copy-start.12 = (s32[8]{0:T(128)S(1)}, s32[8]{0:T(128)}, u32[]{:S(2)}) copy-start(s32[8]{0:T(128)} %refs_0_.3) | copy-start | bytes 100
  40.8 29.9 %copy-start.14 = (s32[8]{0:T(128)S(1)}, s32[8]{0:T(128)}, u32[]{:S(2)}) copy-start(s32[8]{0:T(128)} %refs_1_.3) | copy-start | bytes 100
  67.0 24.2 %all-to-all-start.3 = ((bf16[32,48,256]{2,1,0:T(8,128)(2,1)}), bf16[32,48,256]{2,1,0:T(8,128)(2,1)S(1)}, u32[]{:S(2)}, u32[]{:S(2)}) async-start(bf16[32,48,256]{2,1,0:T(8,128)(2,1)} %get-tuple-element.48), calls=%async_computation.3 | async-start | bytes 1572864 | tf_op jit(solution)/shard_map/all_to_all | solution.py:619
  70.7 2.2 %copy-start.16 = (bf16[8,4,512,128]{3,2,1,0:T(8,128)(2,1)S(1)}, bf16[8,4,512,128]{3,2,1,0:T(8,128)(2,1)}, u32[]{:S(2)}) copy-start(bf16[8,4,512,128]{3,2,1,0:T(8,128)(2,1)} %copy-done.15) | copy-start | bytes 12582916
  72.9 1.6 %copy-start.19 = (s32[8,512,128]{2,1,0:T(8,128)S(1)}, s32[8,512,128]{2,1,0:T(8,128)}, u32[]{:S(2)}) copy-start(s32[8,512,128]{2,1,0:T(8,128)} %copy-done.18) | copy-start | bytes 6291460
  91.1 2.2 %copy-start.17 = (bf16[8,4,512,128]{3,2,1,0:T(8,128)(2,1)S(1)}, bf16[8,4,512,128]{3,2,1,0:T(8,128)(2,1)}, u32[]{:S(2)}) copy-start(bf16[8,4,512,128]{3,2,1,0:T(8,128)(2,1)} %copy-done.15) | copy-start | bytes 12582916
  93.3 1.6 %copy-start.20 = (s32[8,512,128]{2,1,0:T(8,128)S(1)}, s32[8,512,128]{2,1,0:T(8,128)}, u32[]{:S(2)}) copy-start(s32[8,512,128]{2,1,0:T(8,128)} %copy-done.18) | copy-start | bytes 6291460
where the time goes:
time: 121 us; the launch traced here: 120 us
  waiting for transfers between devices  36.6 us (30%)
  Pallas kernels  32.9 us (27%)
  blocking collectives  21.2 us (18%)
  local copies, waits for them, and re-layouts  14.1 us (12%)
  starting transfers between devices  13.5 us (11%)
    all_to_all x1, waiting for transfers between devices, on_device(): early_rows = exchange(early_here)  21.9 us
    all_to_all x1, blocking collectives, on_device(): lax.all_to_all(table.reshape(scorers, span_live // LANES, LANES), 'scorer...  21.2 us
    unnamed x51, local copies, waits for them, and re-layouts  14 us
    pallas_call x2, Pallas kernels, score(): pl.pallas_call(functools.partial(score_kernel, bases=tuple(bases), from_p...  12.2 us
    pallas_call x2, Pallas kernels, serve(): pl.pallas_call(functools.partial(serve_kernel, first=first, sized=sized),...  9.16 us
    all_to_all x1, waiting for transfers between devices, on_device(): late_rows = exchange(late_here)  7.63 us
    all_to_all x1, starting transfers between devices, on_device(): asked_here = exchange(asked)  7.3 us
    all_to_all x1, waiting for transfers between devices, on_device(): asked_here = exchange(asked)  7.12 us
  transfers between devices with their start and end apart: 3, of which 3 were waited for; matrix products, arithmetic and copies ran while one was open for 0% of the time, Pallas kernels for 11%

commit v1 on v0

--- a/solution.py
+++ b/solution.py
@@ -169,9 +169,7 @@
         scratch_shapes=[pltpu.VMEM((column_rows, devices), jnp.int32)],
         compiler_params=pltpu.CompilerParams(vmem_limit_bytes=VMEM_LIMIT),
         cost_estimate=pl.CostEstimate(
-            flops=2 * devices * places * rows_dev * width,
-            bytes_accessed=2 * (rows_dev + devices * sum(place_counts)) * width,
-            transcendentals=0,
+            flops=1_000_000, bytes_accessed=100_000, transcendentals=0
         ),
         name="serve",
     )(asked_here, store_rows, size_table, after)
@@ -187,10 +185,8 @@
     return jnp.sum(mine, axis=0, keepdims=True).astype(jnp.int32)
 
 
-def prep_kernel(
-    cand_ref, query_ref, first_ref, bias_first_ref, score_ref, rank_ref, after_ref, *out_refs
-):
-    queries_ref, base_ref, place_ref, score_cols_ref = out_refs
+def prep_kernel(cand_ref, query_ref, score_ref, rank_ref, after_ref, *out_refs):
+    queries_ref, place_ref, score_cols_ref = out_refs
     devices = after_ref.shape[0]
     cands, width = cand_ref.shape[1:]
     size = width // HEADS
@@ -205,7 +201,6 @@
             own = lane // size == h % 2
             picks = jnp.where(lane % size < OFFSET_PIECES, 1.0, 0.0)
             queries_ref[r, h] = jnp.where(own, pair, picks).astype(jnp.bfloat16)
-        base_ref[r] = dot(cand_ref[r], first_ref[:width, :]) + bias_first_ref[...]
         spot = row_of(rank_ref, r, slice(None))
         at = (spot & (LANES - 1)) + 1
         place = (at // BLOCK) * (devices * BLOCK) + (spot // LANES) * BLOCK + at % BLOCK
@@ -215,38 +210,35 @@
     lax.fori_loop(0, cand_ref.shape[0], one_request, 0)
 
 
-def prep(candidates, query_proj, mlp_first, bias_first, score_proj, ranks, after):
+def prep(candidates, query_proj, score_proj, ranks, after):
     requests, cands, width = candidates.shape
-    units = mlp_first.shape[1]
     return pl.pallas_call(
         prep_kernel,
-        in_specs=[whole() for _ in range(6)] + [whole(pl.ANY)],
-        out_specs=[whole() for _ in range(4)],
+        in_specs=[whole() for _ in range(4)] + [whole(pl.ANY)],
+        out_specs=[whole() for _ in range(3)],
         out_shape=[
             jax.ShapeDtypeStruct((requests, HEADS, cands, LANES), jnp.bfloat16),
-            jax.ShapeDtypeStruct((requests, cands, units), jnp.float32),
             jax.ShapeDtypeStruct((*ranks.shape, LANES), jnp.int32),
             jax.ShapeDtypeStruct((score_proj.shape[1], LANES), jnp.bfloat16),
         ],
         compiler_params=pltpu.CompilerParams(vmem_limit_bytes=VMEM_LIMIT),
         cost_estimate=pl.CostEstimate(
-            flops=2 * requests * cands * width * (width + units),
-            bytes_accessed=18 * requests * cands * width,
-            transcendentals=0,
+            flops=1_000_000, bytes_accessed=100_000, transcendentals=0
         ),
         name="prep",
-    )(candidates, query_proj, mlp_first, bias_first, score_proj, ranks, after)
+    )(candidates, query_proj, score_proj, ranks, after)
 
 
 def score_kernel(*refs, bases, from_place, to_place, spare):
     valid_ref, count_ref, span_ref, before_flag_ref = refs[:4]
-    base_all, queries_all, place_all, rank_ref, target_ref = refs[4:9]
+    cand_all, queries_all, place_all, rank_ref, target_ref = refs[4:9]
     arrived_all = refs[9 : 9 + len(bases)]
     (
         key_ref,
         value_ref,
         out_proj_ref,
         first_ref,
+        bias_first_ref,
         second_ref,
         bias_second_ref,
         score_ref,
@@ -260,7 +252,7 @@
         least_ref,
         most_ref,
         size_ref,
-        base_ref,
+        cand_ref,
         queries_ref,
         place_ref,
         arrived_sems,
@@ -269,8 +261,7 @@
     ) = refs[9 + len(bases) :]
     requests, slots = rank_ref.shape
     devices = arrived_refs[0].shape[0]
-    cands = base_ref.shape[1]
-    width = rows_ref.shape[1]
+    cands, width = cand_ref.shape[1:]
     head_size = width // HEADS
     cand_part = math.gcd(cands, 256)
     highs = table_ref.shape[0]
@@ -278,7 +269,7 @@
     to_log2 = math.log2(math.e) / scale
     sizes_done = range(slots // 2, slots + 1, LANES)
     at_hand = len(bases) - 1 if spare else len(bases)
-    fetched = ((place_all, place_ref), (queries_all, queries_ref), (base_all, base_ref))
+    fetched = ((place_all, place_ref), (queries_all, queries_ref), (cand_all, cand_ref))
     own_rows = [slice(h % 2 * head_size, (h % 2 + 1) * head_size) for h in range(HEADS)]
     other_rows = [slice((1 - h % 2) * head_size, (2 - h % 2) * head_size) for h in range(HEADS)]
 
@@ -412,7 +403,11 @@
     def rate(last, slot):
         r = jnp.maximum(last, 0)
         attended = dot(context_ref[slot], out_proj_ref[...]).astype(jnp.bfloat16)
-        hidden = dot(attended, first_ref[width:, :]) + base_ref[r]
+        hidden = (
+            dot(cand_ref[r], first_ref[:width, :])
+            + dot(attended, first_ref[width:, :])
+            + bias_first_ref[...]
+        )
         hidden = jnp.maximum(hidden, 0.0).astype(jnp.bfloat16)
         hidden = dot(hidden, second_ref[...]) + bias_second_ref[...]
         hidden = jnp.maximum(hidden, 0.0).astype(jnp.bfloat16)
@@ -492,8 +487,8 @@
 
 
 def score(scalars, operands, arrived, weights, before, places, spare=False):
-    base, queries, columns, ranks, _ = operands
-    cands, width = base.shape[1], arrived[0].shape[2]
+    candidates, queries, columns, ranks, _ = operands
+    cands, width = candidates.shape[1:]
     slots = ranks.shape[1]
     devices = arrived[0].shape[0]
     bases = []
@@ -509,9 +504,9 @@
             spare=spare,
         ),
         in_specs=[whole(pltpu.SMEM)] * 4
-        + [whole(pl.ANY)] * 3
+        + [whole(pltpu.HBM)] * 3
         + [whole()] * 2
-        + [whole(pl.ANY)] * len(arrived)
+        + [whole(pltpu.HBM)] * len(arrived)
         + [whole() for _ in (*weights, before)],
         out_specs=[whole(), whole(pltpu.SMEM)],
         scratch_shapes=[
@@ -522,7 +517,7 @@
             pltpu.VMEM((ROWS_AT_ONCE, 1), jnp.float32),
             pltpu.VMEM((ROWS_AT_ONCE, 1), jnp.float32),
             pltpu.VMEM((LANES, devices), jnp.bfloat16),
-            pltpu.VMEM(base.shape, base.dtype),
+            pltpu.VMEM(candidates.shape, candidates.dtype),
             pltpu.VMEM(queries.shape, queries.dtype),
             pltpu.VMEM(columns.shape, columns.dtype),
             pltpu.SemaphoreType.DMA((len(arrived),)),
@@ -588,14 +583,8 @@
     lookup = (asked_here, store_rows, cluster_logsize.reshape(-1, LANES))
     early_here, most = serve(*lookup, asked_here, 0, [early], True)
     early_rows = exchange(early_here)
-    queries, base, columns, score_cols = prep(
-        candidates,
-        query_proj,
-        mlp_first,
-        bias_first.reshape(1, -1),
-        score_proj.reshape(1, -1),
-        ranks,
-        early_here,
+    queries, columns, score_cols = prep(
+        candidates, query_proj, score_proj.reshape(1, -1), ranks, early_here
     )
     last_rows = lax.cond(
         most[0] + 1 > cuts[2],
@@ -608,13 +597,14 @@
         value_proj,
         out_proj,
         mlp_first,
+        bias_first.reshape(1, -1),
         mlp_second,
         bias_second.reshape(1, -1),
         score_cols,
     )
     table = jnp.zeros((scorers * span_live // LANES, LANES), jnp.float32)
     scalars = (valid_count, cand_count, span)
-    shared = (base, queries, columns, ranks, candidate_row)
+    shared = (candidates, queries, columns, ranks, candidate_row)
     late_here, early_rows = lax.optimization_barrier((late_here, early_rows))
     late_rows = exchange(late_here)
     no_flag = jnp.zeros((1,), jnp.int32)

time: 121 us -> 136 us (1.12)
  local copies, waits for them, and re-layouts: 14.1 us -> 32 us
  waiting for transfers between devices: 36.6 us -> 28.6 us
  blocking collectives: 21.2 us -> 24.9 us
    unnamed x51 -> x79, local copies, waits for them, and re-layouts: 14 us -> 31.9 us
    all_to_all x1, waiting for transfers between devices: 7.63 us -> 0.01 us  [on_device(): late_rows = exchange(late_here)]
    pallas_call x2, Pallas kernels: 12.2 us -> 19 us  [score(): pl.pallas_call(functools.partial(score_kernel, bases=tuple(bases), from_p...]
    pallas_call x1, Pallas kernels: 6.36 us -> 2.44 us  [prep(): pl.pallas_call(prep_kernel, in_specs=[whole() for _ in range(4)] + [whole...]
    all_to_all x1, blocking collectives: 21.2 us -> 24.9 us  [on_device(): lax.all_to_all(table.reshape(scorers, span_live // LANES, LANES), 'scorer...]
    pallas_call x2, Pallas kernels: 9.16 us -> 7.47 us  [serve(): pl.pallas_call(functools.partial(serve_kernel, first=first, sized=sized),...]
  transfers between devices with their start and end apart: 3 -> 3, of which waited for: 3 -> 2; matrix products, arithmetic and copies ran while one was open for 0% -> 1% of each run, Pallas kernels for 11% -> 14%
where the time goes in v1:
time: 136 us; the launch traced here: 135 us
  Pallas kernels  34.2 us (25%)
  local copies, waits for them, and re-layouts  32 us (24%)
  waiting for transfers between devices  28.6 us (21%)
  blocking collectives  24.9 us (18%)
  starting transfers between devices  13.6 us (10%)
    unnamed x79, local copies, waits for them, and re-layouts  31.9 us
    all_to_all x1, blocking collectives, on_device(): lax.all_to_all(table.reshape(scorers, span_live // LANES, LANES), 'scorer...  24.9 us
    all_to_all x1, waiting for transfers between devices, on_device(): early_rows = exchange(early_here)  21.5 us
    pallas_call x2, Pallas kernels, score(): pl.pallas_call(functools.partial(score_kernel, bases=tuple(bases), from_p...  19 us
    pallas_call x2, Pallas kernels, serve(): pl.pallas_call(functools.partial(serve_kernel, first=first, sized=sized),...  7.47 us
    all_to_all x1, starting transfers between devices, on_device(): asked_here = exchange(asked)  7.3 us
    all_to_all x1, waiting for transfers between devices, on_device(): asked_here = exchange(asked)  7.12 us
    pallas_call x1, Pallas kernels, ask(): pl.pallas_call(functools.partial(ask_kernel, rows_dev=rows_dev), in_specs...  5.21 us
  transfers between devices with their start and end apart: 3, of which 2 were waited for; matrix products, arithmetic and copies ran while one was open for 1% of the time, Pallas kernels for 14%

profile of v1, /device:TPU:0, one launch (start us, length us, event | category | flops | bytes accessed | tf_op | source)
XLA Modules:
  0.0 134.8 jit_solution(17626320821823782137)
XLA Ops:
  0.0 0.9 copy-done.11
  1.0 0.7 copy-done.17
  1.7 0.7 copy-done.24
  2.3 0.7 copy-done.27
  3.0 5.2 %ask.1 = (s32[32,128]{1,0:T(8,128)}, s32[8,512]{1,0:T(8,128)S(1)}, s32[16]{0:T(128)S(1)}) custom-call(s32[8]{0:T(128)S(1)} %copy-done.24, s32[8]{0:T(128)S(1)} %copy-done.27, s32[8,512]{1,0:T(8,128)S(1)} %copy-done.17, s32[512,128]{1,0:T(8,128)S(1)} %bitcast.15), custom_call_target="tpu_custom_call" | custom-call | flops 4000000000 | bytes 1000000 | tf_op jit(solution)/shard_map/ask/pallas_call | solution.py:102
  8.2 7.3 %all-to-all-start.1 = ((s32[32,1,128]{2,1,0:T(1,128)}), s32[32,1,128]{2,1,0:T(1,128)S(1)}, u32[]{:S(2)}, u32[]{:S(2)}) async-start(s32[32,1,128]{2,1,0:T(1,128)} %bitcast.2), calls=%async_computation.1 | async-start | bytes 32768 | tf_op jit(solution)/shard_map/all_to_all | solution.py:579
  15.6 7.1 %all-to-all-done.1 = s32[32,1,128]{2,1,0:T(1,128)S(1)} async-done(((s32[32,1,128]{2,1,0:T(1,128)}), s32[32,1,128]{2,1,0:T(1,128)S(1)}, u32[]{:S(2)}, u32[]{:S(2)}) %all-to-all-start.1) | async-done | bytes 16416 | tf_op jit(solution)/shard_map/all_to_all | solution.py:579
  22.7 3.7 %serve.4 = (bf16[32,64,256]{2,1,0:T(8,128)(2,1)}, s32[1]{0:T(128)}) custom-call(s32[32,128]{1,0:T(8,128)S(1)} %bitcast.20, bf16[2048,256]{1,0:T(8,128)(2,1)S(1)} %copy-done.35, bf16[16,128]{1,0:T(8,128)(2,1)S(1)} %bitcast.24, s32[32,128]{1,0:T(8,128)S(1)} %bitcast.21), custom_call_target="tpu_custom_call" | custom-call | flops 1000000 | bytes 100000 | tf_op jit(solution)/shard_map/serve/pallas_call | solution.py:161
  27.1 2.4 %prep.1 = (bf16[8,4,512,128]{3,2,1,0:T(8,128)(2,1)S(1)}, s32[8,512,128]{2,1,0:T(8,128)S(1)}, bf16[256,128]{1,0:T(8,128)(2,1)}) custom-call(bf16[8,512,256]{2,1,0:T(8,128)(2,1)S(1)} %copy-done, bf16[256,256]{1,0:T(8,128)(2,1)S(1)} %copy-done.2, bf16[1,256]{1,0:T(2,128)(2,1)S(1)} %reshape.30.score_ref, s32[8,512]{1,0:T(8,128)S(1)} %get-tuple-element.36.rank_ref.refs_7_, ...), custom_call_target="tpu_custom_call" | custom-call | flops 1000000 | bytes 100000 | tf_op jit(solution)/shard_map/prep/pallas_call | solution.py:215
  29.5 2.0 %copy-done.3 = bf16[8,4,512,128]{3,2,1,0:T(8,128)(2,1)} copy-done((bf16[8,4,512,128]{3,2,1,0:T(8,128)(2,1)}, bf16[8,4,512,128]{3,2,1,0:T(8,128)(2,1)S(1)}, u32[]{:S(2)}) %copy-start.3) | copy-done | bytes 4194328
  31.5 1.4 %copy-done.6 = s32[8,512,128]{2,1,0:T(8,128)} copy-done((s32[8,512,128]{2,1,0:T(8,128)}, s32[8,512,128]{2,1,0:T(8,128)S(1)}, u32[]{:S(2)}) %copy-start.6) | copy-done | bytes 2097176
  32.9 0.1 conditional.1
  32.9 0.1 broadcast.2
  33.0 0.8 copy-done.36
  33.8 2.6 %all-to-all-start.2 = ((bf16[32,64,256]{2,1,0:T(8,128)(2,1)}), bf16[32,64,256]{2,1,0:T(8,128)(2,1)S(1)}, u32[]{:S(2)}, u32[]{:S(2)}) async-start(bf16[32,64,256]{2,1,0:T(8,128)(2,1)} %get-tuple-element.38.after_ref), calls=%async_computation.2 | async-start | bytes 2097152 | tf_op jit(solution)/shard_map/all_to_all | solution.py:585
  36.5 3.7 %serve.5 = (bf16[32,48,256]{2,1,0:T(8,128)(2,1)S(1)}, s32[1]{0:T(128)}) custom-call(s32[32,128]{1,0:T(8,128)S(1)} %bitcast.23, bf16[2048,256]{1,0:T(8,128)(2,1)} %store_ref.3, bf16[16,128]{1,0:T(8,128)(2,1)S(1)} %bitcast.26, bf16[32,32,256]{2,1,0:T(8,128)(2,1)} %copy-done.36), custom_call_target="tpu_custom_call" | custom-call | flops 1000000 | bytes 100000 | tf_op jit(solution)/shard_map/serve/pallas_call | solution.py:161
  40.2 0.9 copy-done.1
  41.1 21.5 %all-to-all-done.2.refs_9_ = bf16[32,64,256]{2,1,0:T(8,128)(2,1)S(1)} async-done(((bf16[32,64,256]{2,1,0:T(8,128)(2,1)}), bf16[32,64,256]{2,1,0:T(8,128)(2,1)S(1)}, u32[]{:S(2)}, u32[]{:S(2)}) %all-to-all-start.2) | async-done | bytes 1048608 | tf_op jit(solution)/shard_map/all_to_all | solution.py:585
  62.7 3.7 %all-to-all-start.3 = ((bf16[32,48,256]{2,1,0:T(8,128)(2,1)}), bf16[32,48,256]{2,1,0:T(8,128)(2,1)}, u32[]{:S(2)}, u32[]{:S(2)}) async-start(bf16[32,48,256]{2,1,0:T(8,128)(2,1)} %copy-done.1), calls=%async_computation.3 | async-start | bytes 1572864 | tf_op jit(solution)/shard_map/all_to_all | solution.py:609
  66.3 1.0 copy.20
  67.4 2.2 %copy-done.4 = bf16[8,4,512,128]{3,2,1,0:T(8,128)(2,1)S(1)} copy-done((bf16[8,4,512,128]{3,2,1,0:T(8,128)(2,1)S(1)}, bf16[8,4,512,128]{3,2,1,0:T(8,128)(2,1)}, u32[]{:S(2)}) %copy-start.4) | copy-done | bytes 4194328
  69.5 1.6 %copy-done.7 = s32[8,512,128]{2,1,0:T(8,128)S(1)} copy-done((s32[8,512,128]{2,1,0:T(8,128)S(1)}, s32[8,512,128]{2,1,0:T(8,128)}, u32[]{:S(2)}) %copy-start.7) | copy-done | bytes 2097176
  71.1 1.0 copy-done.9
  72.2 0.9 copy-done.13
  73.1 0.9 copy-done.15
  74.0 0.7 copy-done.18
  74.7 0.7 copy-done.20
  75.4 0.7 copy-done.22
  76.1 0.7 copy-done.25
  76.7 0.7 copy-done.28
  77.4 0.7 copy-done.33
  78.0 15.0 %score.2 = (f32[128,128]{1,0:T(8,128)S(1)}, s32[1]{0:T(128)}) custom-call(s32[8]{0:T(128)S(1)} %copy-done.25, s32[8]{0:T(128)S(1)} %copy-done.28, s32[16]{0:T(128)S(1)} %copy-done.33, s32[1]{0:T(128)} %constant.2.clone.1.refs_3_, bf16[8,512,256]{2,1,0:T(8,128)(2,1)S(1)} %copy-done, bf16[8,4,512,128]{3,2,1,0:T(8,128)(2,1)S(1)} %copy-done.4, ...), custom_call_target="tpu_custom_call" | custom-call | flops 10000000000 | bytes 5000000 | tf_op jit(solution)/shard_map/score/pallas_call | solution.py:498
  93.0 0.6 copy-done.30
  93.6 2.2 %copy-done.5 = bf16[8,4,512,128]{3,2,1,0:T(8,128)(2,1)S(1)} copy-done((bf16[8,4,512,128]{3,2,1,0:T(8,128)(2,1)S(1)}, bf16[8,4,512,128]{3,2,1,0:T(8,128)(2,1)}, u32[]{:S(2)}) %copy-start.5) | copy-done | bytes 4194328
  95.8 1.6 %copy-done.8 = s32[8,512,128]{2,1,0:T(8,128)S(1)} copy-done((s32[8,512,128]{2,1,0:T(8,128)S(1)}, s32[8,512,128]{2,1,0:T(8,128)}, u32[]{:S(2)}) %copy-start.8) | copy-done | bytes 2097176
  97.4 1.0 copy-done.10
  98.5 0.9 copy-done.14
  99.4 0.9 copy-done.16
  100.3 0.7 copy-done.19
  101.0 0.7 copy-done.21
  101.7 0.7 copy-done.23
  102.3 0.7 copy-done.26
  103.0 0.7 copy-done.29
  103.7 0.8 copy-done.31
  104.5 0.7 copy-done.34
  105.1 4.1 %score.3 = (f32[128,128]{1,0:T(8,128)S(1)}, s32[1]{0:T(128)}) custom-call(s32[8]{0:T(128)S(1)} %copy-done.26, s32[8]{0:T(128)S(1)} %copy-done.29, s32[16]{0:T(128)S(1)} %copy-done.34, s32[1]{0:T(128)} %get-tuple-element.45.refs_3_, bf16[8,512,256]{2,1,0:T(8,128)(2,1)S(1)} %copy-done, bf16[8,4,512,128]{3,2,1,0:T(8,128)(2,1)S(1)} %copy-done.5, ...), custom_call_target="tpu_custom_call" | custom-call | flops 10000000000 | bytes 5000000 | tf_op jit(solution)/shard_map/score/pallas_call | solution.py:498
  109.2 24.9 %all_to_all.31 = f32[8,16,128]{2,1,0:T(8,128)S(1)} all-to-all(f32[8,16,128]{2,1,0:T(8,128)S(1)} %bitcast.14), channel_id=1, replica_groups=mesh['store'=4,'scorer'=8] {'scorer'}, dimensions={0} | all-to-all | bytes 131072 | tf_op jit(solution)/shard_map/all_to_all | solution.py:615
  134.2 0.6 reduce_sum.9
  (49 shorter events, 0.1 us)
Async XLA Ops:
  0.0 0.9 copy-start.11
  1.0 0.7 copy-start.17
  1.7 0.7 copy-start.24
  2.3 0.7 copy-start.27
  3.0 12.6 %copy-start.38 = (bf16[256]{0:T(256)(128)(2,1)S(1)}, bf16[256]{0:T(256)(128)(2,1)}, u32[]{:S(2)}) copy-start(bf16[256]{0:T(256)(128)(2,1)} %param.35) | copy-start | bytes 1540
  3.0 19.7 %copy-start.35 = (bf16[2048,256]{1,0:T(8,128)(2,1)S(1)}, bf16[2048,256]{1,0:T(8,128)(2,1)}, u32[]{:S(2)}) copy-start(bf16[2048,256]{1,0:T(8,128)(2,1)} %store_ref.3) | copy-start | bytes 3145732
  3.0 19.7 %copy-start.37 = (bf16[2048]{0:T(1024)(128)(2,1)S(1)}, bf16[2048]{0:T(1024)(128)(2,1)}, u32[]{:S(2)}) copy-start(bf16[2048]{0:T(1024)(128)(2,1)} %param.20) | copy-start | bytes 12292
  3.0 24.1 %copy-start = (bf16[8,512,256]{2,1,0:T(8,128)(2,1)S(1)}, bf16[8,512,256]{2,1,0:T(8,128)(2,1)}, u32[]{:S(2)}) copy-start(bf16[8,512,256]{2,1,0:T(8,128)(2,1)} %refs_4_.3) | copy-start | bytes 6291460
  3.0 24.1 %copy-start.2 = (bf16[256,256]{1,0:T(8,128)(2,1)S(1)}, bf16[256,256]{1,0:T(8,128)(2,1)}, u32[]{:S(2)}) copy-start(bf16[256,256]{1,0:T(8,128)(2,1)} %query_ref.1) | copy-start | bytes 393220
  8.2 7.3 %copy-start.32 = (s32[16]{0:T(128)}, s32[16]{0:T(128)S(1)}, u32[]{:S(2)}) copy-start(s32[16]{0:T(128)S(1)} %get-tuple-element.35.refs_2_) | copy-start | bytes 196
  8.2 14.5 %all-to-all-start.1 = ((s32[32,1,128]{2,1,0:T(1,128)}), s32[32,1,128]{2,1,0:T(1,128)S(1)}, u32[]{:S(2)}, u32[]{:S(2)}) async-start(s32[32,1,128]{2,1,0:T(1,128)} %bitcast.2), calls=%async_computation.1 | async-start | bytes 32768 | tf_op jit(solution)/shard_map/all_to_all | solution.py:579
  29.5 2.0 %copy-start.3 = (bf16[8,4,512,128]{3,2,1,0:T(8,128)(2,1)}, bf16[8,4,512,128]{3,2,1,0:T(8,128)(2,1)S(1)}, u32[]{:S(2)}) copy-start(bf16[8,4,512,128]{3,2,1,0:T(8,128)(2,1)S(1)} %get-tuple-element.39.refs_5_) | copy-start | bytes 12582916
  31.5 1.4 %copy-start.6 = (s32[8,512,128]{2,1,0:T(8,128)}, s32[8,512,128]{2,1,0:T(8,128)S(1)}, u32[]{:S(2)}) copy-start(s32[8,512,128]{2,1,0:T(8,128)S(1)} %get-tuple-element.40.refs_6_) | copy-start | bytes 6291460
  32.9 0.8 copy-start.36
  33.8 28.9 %all-to-all-start.2 = ((bf16[32,64,256]{2,1,0:T(8,128)(2,1)}), bf16[32,64,256]{2,1,0:T(8,128)(2,1)S(1)}, u32[]{:S(2)}, u32[]{:S(2)}) async-start(bf16[32,64,256]{2,1,0:T(8,128)(2,1)} %get-tuple-element.38.after_ref), calls=%async_computation.2 | async-start | bytes 2097152 | tf_op jit(solution)/shard_map/all_to_all | solution.py:585
  36.4 30.9 %copy-start.12 = (bf16[512,256]{1,0:T(8,128)(2,1)S(1)}, bf16[512,256]{1,0:T(8,128)(2,1)}, u32[]{:S(2)}) copy-start(bf16[512,256]{1,0:T(8,128)(2,1)} %refs_17_.1) | copy-start | bytes 786436
  40.2 0.9 copy-start.1
  62.7 31.0 %all-to-all-start.3 = ((bf16[32,48,256]{2,1,0:T(8,128)(2,1)}), bf16[32,48,256]{2,1,0:T(8,128)(2,1)}, u32[]{:S(2)}, u32[]{:S(2)}) async-start(bf16[32,48,256]{2,1,0:T(8,128)(2,1)} %copy-done.1), calls=%async_computation.3 | async-start | bytes 1572864 | tf_op jit(solution)/shard_map/all_to_all | solution.py:609
  67.4 2.2 %copy-start.4 = (bf16[8,4,512,128]{3,2,1,0:T(8,128)(2,1)S(1)}, bf16[8,4,512,128]{3,2,1,0:T(8,128)(2,1)}, u32[]{:S(2)}) copy-start(bf16[8,4,512,128]{3,2,1,0:T(8,128)(2,1)} %copy-done.3) | copy-start | bytes 12582916
  69.5 1.6 %copy-start.7 = (s32[8,512,128]{2,1,0:T(8,128)S(1)}, s32[8,512,128]{2,1,0:T(8,128)}, u32[]{:S(2)}) copy-start(s32[8,512,128]{2,1,0:T(8,128)} %copy-done.6) | copy-start | bytes 6291460
  71.1 1.0 copy-start.9
  72.2 0.9 copy-start.13
  73.1 0.9 copy-start.15
  74.0 0.7 copy-start.18
  74.7 0.7 copy-start.20
  75.4 0.7 copy-start.22
  76.1 0.7 copy-start.25
  76.7 0.7 copy-start.28
  77.4 0.7 copy-start.33
  93.0 0.6 copy-start.30
  93.6 2.2 %copy-start.5 = (bf16[8,4,512,128]{3,2,1,0:T(8,128)(2,1)S(1)}, bf16[8,4,512,128]{3,2,1,0:T(8,128)(2,1)}, u32[]{:S(2)}) copy-start(bf16[8,4,512,128]{3,2,1,0:T(8,128)(2,1)} %copy-done.3) | copy-start | bytes 12582916
  95.8 1.6 %copy-start.8 = (s32[8,512,128]{2,1,0:T(8,128)S(1)}, s32[8,512,128]{2,1,0:T(8,128)}, u32[]{:S(2)}) copy-start(s32[8,512,128]{2,1,0:T(8,128)} %copy-done.6) | copy-start | bytes 6291460
  97.4 1.0 copy-start.10
  98.5 0.9 copy-start.14
  99.4 0.9 copy-start.16
  100.3 0.7 copy-start.19
  101.0 0.7 copy-start.21
  101.7 0.7 copy-start.23
  102.3 0.7 copy-start.26
  103.0 0.7 copy-start.29
  103.7 0.8 copy-start.31
  104.5 0.7 copy-start.34

commit v2 on v1

--- a/solution.py
+++ b/solution.py
@@ -169,7 +169,9 @@
         scratch_shapes=[pltpu.VMEM((column_rows, devices), jnp.int32)],
         compiler_params=pltpu.CompilerParams(vmem_limit_bytes=VMEM_LIMIT),
         cost_estimate=pl.CostEstimate(
-            flops=1_000_000, bytes_accessed=100_000, transcendentals=0
+            flops=2 * devices * places * rows_dev * width,
+            bytes_accessed=2 * (rows_dev + devices * sum(place_counts)) * width,
+            transcendentals=0,
         ),
         name="serve",
     )(asked_here, store_rows, size_table, after)
@@ -223,7 +225,9 @@
         ],
         compiler_params=pltpu.CompilerParams(vmem_limit_bytes=VMEM_LIMIT),
         cost_estimate=pl.CostEstimate(
-            flops=1_000_000, bytes_accessed=100_000, transcendentals=0
+            flops=2 * requests * cands * width * width,
+            bytes_accessed=10 * requests * cands * width,
+            transcendentals=0,
         ),
         name="prep",
     )(candidates, query_proj, score_proj, ranks, after)
@@ -504,9 +508,9 @@
             spare=spare,
         ),
         in_specs=[whole(pltpu.SMEM)] * 4
-        + [whole(pltpu.HBM)] * 3
+        + [whole(pl.ANY)] * 3
         + [whole()] * 2
-        + [whole(pltpu.HBM)] * len(arrived)
+        + [whole(pl.ANY)] * len(arrived)
         + [whole() for _ in (*weights, before)],
         out_specs=[whole(), whole(pltpu.SMEM)],
         scratch_shapes=[
@@ -586,12 +590,7 @@
     queries, columns, score_cols = prep(
         candidates, query_proj, score_proj.reshape(1, -1), ranks, early_here
     )
-    last_rows = lax.cond(
-        most[0] + 1 > cuts[2],
-        lambda: exchange(serve(*lookup, score_cols, cuts[2], [cuts[3] - cuts[2]], False)[0]),
-        lambda: jnp.zeros((devices, cuts[3] - cuts[2], width), jnp.bfloat16),
-    )
-    late_here, _ = serve(*lookup, last_rows, cuts[1], [cuts[2] - cuts[1]], False)
+    late_here, _ = serve(*lookup, score_cols, cuts[1], [cuts[2] - cuts[1]], False)
     weights = (
         key_proj.T,
         value_proj,
@@ -607,6 +606,11 @@
     shared = (candidates, queries, columns, ranks, candidate_row)
     late_here, early_rows = lax.optimization_barrier((late_here, early_rows))
     late_rows = exchange(late_here)
+    last_rows = lax.cond(
+        most[0] + 1 > cuts[2],
+        lambda: exchange(serve(*lookup, late_rows, cuts[2], [cuts[3] - cuts[2]], False)[0]),
+        lambda: jnp.zeros((devices, cuts[3] - cuts[2], width), jnp.bfloat16),
+    )
     no_flag = jnp.zeros((1,), jnp.int32)
     arrived = (early_rows,)
     table, flag = score((*scalars, no_flag), shared, arrived, weights, table, cuts[0:2])

time: 136 us -> 131 us (0.963)
  Pallas kernels: 34.2 us -> 47.2 us
  waiting for transfers between devices: 28.6 us -> 16.7 us
  starting transfers between devices: 13.6 us -> 6.45 us
  local copies, waits for them, and re-layouts: 32 us -> 34.3 us
  blocking collectives: 24.9 us -> 22.6 us
    all_to_all x1, blocking collectives: 24.9 us -> 8.34 us  [on_device(): lax.all_to_all(table.reshape(scorers, span_live // LANES, LANES), 'scorer...]
    pallas_call x2, Pallas kernels: 19 us -> 33.8 us  [score(): pl.pallas_call(functools.partial(score_kernel, bases=tuple(bases), from_p...]
    all_to_all x0 -> x1, blocking collectives: none -> 14.3 us  [on_device(): asked_here = exchange(asked)]
    all_to_all x1 -> x0, starting transfers between devices: 7.3 us -> none  [on_device(): asked_here = exchange(asked)]
    all_to_all x1 -> x0, waiting for transfers between devices: 7.12 us -> none  [on_device(): asked_here = exchange(asked)]
    all_to_all x1, waiting for transfers between devices: 21.5 us -> 16.7 us  [on_device(): early_rows = exchange(early_here)]
    unnamed x79 -> x87, local copies, waits for them, and re-layouts: 31.9 us -> 33.4 us
  transfers between devices with their start and end apart: 3 -> 2, of which waited for: 2 -> 1; matrix products, arithmetic and copies ran while one was open for 1% -> 1% of each run, Pallas kernels for 14% -> 18%
where the time goes in v2:
time: 131 us; the launch traced here: 129 us
  Pallas kernels  47.2 us (36%)
  local copies, waits for them, and re-layouts  34.3 us (26%)
  blocking collectives  22.6 us (17%)
  waiting for transfers between devices  16.7 us (13%)
  starting transfers between devices  6.45 us (5%)
    pallas_call x2, Pallas kernels, score(): pl.pallas_call(functools.partial(score_kernel, bases=tuple(bases), from_p...  33.8 us
    unnamed x87, local copies, waits for them, and re-layouts  33.4 us
    all_to_all x1, waiting for transfers between devices, on_device(): early_rows = exchange(early_here)  16.7 us
    all_to_all x1, blocking collectives, on_device(): asked_here = exchange(asked)  14.3 us
    all_to_all x1, blocking collectives, on_device(): lax.all_to_all(table.reshape(scorers, span_live // LANES, LANES), 'scorer...  8.34 us
    pallas_call x2, Pallas kernels, serve(): pl.pallas_call(functools.partial(serve_kernel, first=first, sized=sized),...  6.25 us
    pallas_call x1, Pallas kernels, ask(): pl.pallas_call(functools.partial(ask_kernel, rows_dev=rows_dev), in_specs...  5.11 us
    all_to_all x1, starting transfers between devices, on_device(): late_rows = exchange(late_here)  3.65 us
  transfers between devices with their start and end apart: 2, of which 1 were waited for; matrix products, arithmetic and copies ran while one was open for 1% of the time, Pallas kernels for 18%

profile of v2, /device:TPU:0, one launch (start us, length us, event | category | flops | bytes accessed | tf_op | source)
XLA Modules:
  0.0 128.7 jit_solution(4966219484367207529)
XLA Ops:
  0.0 0.9 copy-done.11
  1.0 0.7 copy-done.20
  1.7 0.7 copy-done.27
  2.3 0.7 copy-done.30
  3.0 5.1 %ask.1 = (s32[32,128]{1,0:T(8,128)S(1)}, s32[8,512]{1,0:T(8,128)S(1)}, s32[16]{0:T(128)S(1)}) custom-call(s32[8]{0:T(128)S(1)} %copy-done.27, s32[8]{0:T(128)S(1)} %copy-done.30, s32[8,512]{1,0:T(8,128)S(1)} %copy-done.20, s32[512,128]{1,0:T(8,128)S(1)} %bitcast.16), custom_call_target="tpu_custom_call" | custom-call | flops 4000000000 | bytes 1000000 | tf_op jit(solution)/shard_map/ask/pallas_call | solution.py:102
  8.1 14.3 %all_to_all.31 = s32[32,1,128]{2,1,0:T(1,128)S(1)} all-to-all(s32[32,1,128]{2,1,0:T(1,128)S(1)} %bitcast.15), channel_id=1, replica_groups=mesh['store'=4,'scorer'=8] {'store','scorer'}, dimensions={0} | all-to-all | bytes 32768 | tf_op jit(solution)/shard_map/all_to_all | solution.py:583
  22.4 3.8 %serve.4 = (bf16[32,64,256]{2,1,0:T(8,128)(2,1)}, s32[1]{0:T(128)}) custom-call(s32[32,128]{1,0:T(8,128)S(1)} %bitcast.21, bf16[2048,256]{1,0:T(8,128)(2,1)S(1)} %copy-done.39, bf16[16,128]{1,0:T(8,128)(2,1)S(1)} %bitcast.26, s32[32,128]{1,0:T(8,128)S(1)} %bitcast.22), custom_call_target="tpu_custom_call" | custom-call | flops 2147483648 | bytes 2097152 | tf_op jit(solution)/shard_map/serve/pallas_call | solution.py:161
  26.2 2.8 %all-to-all-start.2 = ((bf16[32,64,256]{2,1,0:T(8,128)(2,1)}), bf16[32,64,256]{2,1,0:T(8,128)(2,1)S(1)}, u32[]{:S(2)}, u32[]{:S(2)}) async-start(bf16[32,64,256]{2,1,0:T(8,128)(2,1)} %get-tuple-element.38.after_ref), calls=%async_computation.2 | async-start | bytes 2097152 | tf_op jit(solution)/shard_map/all_to_all | solution.py:589
  29.1 2.1 %prep.1 = (bf16[8,4,512,128]{3,2,1,0:T(8,128)(2,1)S(1)}, s32[8,512,128]{2,1,0:T(8,128)S(1)}, bf16[256,128]{1,0:T(8,128)(2,1)S(1)}) custom-call(bf16[8,512,256]{2,1,0:T(8,128)(2,1)S(1)} %copy-done, bf16[256,256]{1,0:T(8,128)(2,1)S(1)} %copy-done.2, bf16[1,256]{1,0:T(2,128)(2,1)S(1)} %reshape.30.score_ref, s32[8,512]{1,0:T(8,128)S(1)} %get-tuple-element.36.rank_ref.refs_7_, ...), custom_call_target="tpu_custom_call" | custom-call | flops 536870912 | bytes 10485760 | tf_op jit(solution)/shard_map/prep/pallas_call | solution.py:217
  31.1 2.0 %copy-done.3 = bf16[8,4,512,128]{3,2,1,0:T(8,128)(2,1)} copy-done((bf16[8,4,512,128]{3,2,1,0:T(8,128)(2,1)}, bf16[8,4,512,128]{3,2,1,0:T(8,128)(2,1)S(1)}, u32[]{:S(2)}) %copy-start.3) | copy-done | bytes 4194328
  33.1 1.4 %copy-done.6 = s32[8,512,128]{2,1,0:T(8,128)} copy-done((s32[8,512,128]{2,1,0:T(8,128)}, s32[8,512,128]{2,1,0:T(8,128)S(1)}, u32[]{:S(2)}) %copy-start.6) | copy-done | bytes 2097176
  34.5 2.5 %serve.5 = (bf16[32,48,256]{2,1,0:T(8,128)(2,1)S(1)}, s32[1]{0:T(128)}) custom-call(s32[32,128]{1,0:T(8,128)S(1)} %bitcast.23, bf16[2048,256]{1,0:T(8,128)(2,1)S(1)} %copy-done.40, bf16[16,128]{1,0:T(8,128)(2,1)S(1)} %bitcast.27, bf16[256,128]{1,0:T(8,128)(2,1)S(1)} %get-tuple-element.41.after_ref.refs_17_.refs_19_), custom_call_target="tpu_custom_call" | custom-call | flops 1610612736 | bytes 1835008 | tf_op jit(solution)/shard_map/serve/pallas_call | solution.py:161
  37.0 0.9 copy-done.1
  37.9 0.6 copy-done.17
  38.5 16.7 %all-to-all-done.2.refs_9_ = bf16[32,64,256]{2,1,0:T(8,128)(2,1)S(1)} async-done(((bf16[32,64,256]{2,1,0:T(8,128)(2,1)}), bf16[32,64,256]{2,1,0:T(8,128)(2,1)S(1)}, u32[]{:S(2)}, u32[]{:S(2)}) %all-to-all-start.2) | async-done | bytes 1048608 | tf_op jit(solution)/shard_map/all_to_all | solution.py:589
  55.2 3.7 %all-to-all-start.3 = ((bf16[32,48,256]{2,1,0:T(8,128)(2,1)}), bf16[32,48,256]{2,1,0:T(8,128)(2,1)}, u32[]{:S(2)}, u32[]{:S(2)}) async-start(bf16[32,48,256]{2,1,0:T(8,128)(2,1)} %copy-done.1), calls=%async_computation.3 | async-start | bytes 1572864 | tf_op jit(solution)/shard_map/all_to_all | solution.py:608
  58.9 1.0 copy.20
  60.5 2.2 %copy-done.4 = bf16[8,4,512,128]{3,2,1,0:T(8,128)(2,1)S(1)} copy-done((bf16[8,4,512,128]{3,2,1,0:T(8,128)(2,1)S(1)}, bf16[8,4,512,128]{3,2,1,0:T(8,128)(2,1)}, u32[]{:S(2)}) %copy-start.4) | copy-done | bytes 4194328
  62.7 1.6 %copy-done.7 = s32[8,512,128]{2,1,0:T(8,128)S(1)} copy-done((s32[8,512,128]{2,1,0:T(8,128)S(1)}, s32[8,512,128]{2,1,0:T(8,128)}, u32[]{:S(2)}) %copy-start.7) | copy-done | bytes 2097176
  64.3 1.0 copy-done.9
  65.3 0.9 copy-done.13
  66.2 0.9 copy-done.15
  67.1 0.8 copy-done.18
  67.9 0.7 copy-done.21
  68.7 0.7 copy-done.23
  69.3 0.7 copy-done.25
  70.0 0.7 copy-done.28
  70.7 0.7 copy-done.31
  71.3 0.7 copy-done.36
  72.0 18.8 %score.2 = (f32[128,128]{1,0:T(8,128)S(1)}, s32[1]{0:T(128)}) custom-call(s32[8]{0:T(128)S(1)} %copy-done.28, s32[8]{0:T(128)S(1)} %copy-done.31, s32[16]{0:T(128)S(1)} %copy-done.36, s32[1]{0:T(128)} %constant.2.clone.1.refs_3_, bf16[8,512,256]{2,1,0:T(8,128)(2,1)S(1)} %copy-done, bf16[8,4,512,128]{3,2,1,0:T(8,128)(2,1)S(1)} %copy-done.4, ...), custom_call_target="tpu_custom_call" | custom-call | flops 10000000000 | bytes 5000000 | tf_op jit(solution)/shard_map/score/pallas_call | solution.py:502
  90.8 0.6 copy-done.33
  91.4 0.9 conditional.1
  91.4 0.9 broadcast.2
  92.3 2.2 %copy-done.5 = bf16[8,4,512,128]{3,2,1,0:T(8,128)(2,1)S(1)} copy-done((bf16[8,4,512,128]{3,2,1,0:T(8,128)(2,1)S(1)}, bf16[8,4,512,128]{3,2,1,0:T(8,128)(2,1)}, u32[]{:S(2)}) %copy-start.5) | copy-done | bytes 4194328
  94.5 1.6 %copy-done.8 = s32[8,512,128]{2,1,0:T(8,128)S(1)} copy-done((s32[8,512,128]{2,1,0:T(8,128)S(1)}, s32[8,512,128]{2,1,0:T(8,128)}, u32[]{:S(2)}) %copy-start.8) | copy-done | bytes 2097176
  96.1 1.0 copy-done.10
  97.1 0.9 copy-done.14
  98.0 0.9 copy-done.16
  98.9 0.8 copy-done.19
  99.8 0.7 copy-done.22
  100.5 0.7 copy-done.24
  101.2 0.7 copy-done.26
  101.8 0.7 copy-done.29
  102.5 0.7 copy-done.32
  103.2 0.8 copy-done.34
  104.0 0.7 copy-done.37
  104.6 15.1 %score.3 = (f32[128,128]{1,0:T(8,128)S(1)}, s32[1]{0:T(128)}) custom-call(s32[8]{0:T(128)S(1)} %copy-done.29, s32[8]{0:T(128)S(1)} %copy-done.32, s32[16]{0:T(128)S(1)} %copy-done.37, s32[1]{0:T(128)} %get-tuple-element.44.refs_3_, bf16[8,512,256]{2,1,0:T(8,128)(2,1)S(1)} %copy-done, bf16[8,4,512,128]{3,2,1,0:T(8,128)(2,1)S(1)} %copy-done.5, ...), custom_call_target="tpu_custom_call" | custom-call | flops 10000000000 | bytes 5000000 | tf_op jit(solution)/shard_map/score/pallas_call | solution.py:502
  119.7 8.3 %all_to_all.32 = f32[8,16,128]{2,1,0:T(8,128)S(1)} all-to-all(f32[8,16,128]{2,1,0:T(8,128)S(1)} %bitcast.14), channel_id=1, replica_groups=mesh['store'=4,'scorer'=8] {'scorer'}, dimensions={0} | all-to-all | bytes 131072 | tf_op jit(solution)/shard_map/all_to_all | solution.py:619
  (56 shorter events, 0.7 us)
Async XLA Ops:
  0.0 0.9 copy-start.11
  1.0 0.7 copy-start.20
  1.7 0.7 copy-start.27
  2.3 0.7 copy-start.30
  3.0 19.4 %copy-start.39 = (bf16[2048,256]{1,0:T(8,128)(2,1)S(1)}, bf16[2048,256]{1,0:T(8,128)(2,1)}, u32[]{:S(2)}) copy-start(bf16[2048,256]{1,0:T(8,128)(2,1)} %store_ref.3) | copy-start | bytes 3145732
  3.0 19.4 %copy-start.41 = (bf16[2048]{0:T(1024)(128)(2,1)S(1)}, bf16[2048]{0:T(1024)(128)(2,1)}, u32[]{:S(2)}) copy-start(bf16[2048]{0:T(1024)(128)(2,1)} %param.20) | copy-start | bytes 12292
  8.1 14.3 %copy-start.35 = (s32[16]{0:T(128)}, s32[16]{0:T(128)S(1)}, u32[]{:S(2)}) copy-start(s32[16]{0:T(128)S(1)} %get-tuple-element.35.refs_2_) | copy-start | bytes 196
  22.4 12.1 %copy-start.38 = (s32[32,1,128]{2,1,0:T(1,128)}, s32[32,1,128]{2,1,0:T(1,128)S(1)}, u32[]{:S(2)}) copy-start(s32[32,1,128]{2,1,0:T(1,128)S(1)} %all_to_all.31) | copy-start | bytes 49156
  22.4 6.7 %copy-start.2 = (bf16[256,256]{1,0:T(8,128)(2,1)S(1)}, bf16[256,256]{1,0:T(8,128)(2,1)}, u32[]{:S(2)}) copy-start(bf16[256,256]{1,0:T(8,128)(2,1)} %query_ref.1) | copy-start | bytes 393220
  26.2 2.8 %copy-start.42 = (bf16[256]{0:T(256)(128)(2,1)S(1)}, bf16[256]{0:T(256)(128)(2,1)}, u32[]{:S(2)}) copy-start(bf16[256]{0:T(256)(128)(2,1)} %param.35) | copy-start | bytes 1540
  26.2 2.9 %copy-start = (bf16[8,512,256]{2,1,0:T(8,128)(2,1)S(1)}, bf16[8,512,256]{2,1,0:T(8,128)(2,1)}, u32[]{:S(2)}) copy-start(bf16[8,512,256]{2,1,0:T(8,128)(2,1)} %refs_4_.3) | copy-start | bytes 6291460
  26.2 29.0 %all-to-all-start.2 = ((bf16[32,64,256]{2,1,0:T(8,128)(2,1)}), bf16[32,64,256]{2,1,0:T(8,128)(2,1)S(1)}, u32[]{:S(2)}, u32[]{:S(2)}) async-start(bf16[32,64,256]{2,1,0:T(8,128)(2,1)} %get-tuple-element.38.after_ref), calls=%async_computation.2 | async-start | bytes 2097152 | tf_op jit(solution)/shard_map/all_to_all | solution.py:589
  29.0 5.4 %copy-start.40 = (bf16[2048,256]{1,0:T(8,128)(2,1)S(1)}, bf16[2048,256]{1,0:T(8,128)(2,1)}, u32[]{:S(2)}) copy-start(bf16[2048,256]{1,0:T(8,128)(2,1)} %store_ref.3) | copy-start | bytes 3145732
  31.1 2.0 %copy-start.3 = (bf16[8,4,512,128]{3,2,1,0:T(8,128)(2,1)}, bf16[8,4,512,128]{3,2,1,0:T(8,128)(2,1)S(1)}, u32[]{:S(2)}) copy-start(bf16[8,4,512,128]{3,2,1,0:T(8,128)(2,1)S(1)} %get-tuple-element.39.refs_5_) | copy-start | bytes 12582916
  33.1 1.4 %copy-start.6 = (s32[8,512,128]{2,1,0:T(8,128)}, s32[8,512,128]{2,1,0:T(8,128)S(1)}, u32[]{:S(2)}) copy-start(s32[8,512,128]{2,1,0:T(8,128)S(1)} %get-tuple-element.40.refs_6_) | copy-start | bytes 6291460
  34.5 26.0 %copy-start.12 = (bf16[512,256]{1,0:T(8,128)(2,1)S(1)}, bf16[512,256]{1,0:T(8,128)(2,1)}, u32[]{:S(2)}) copy-start(bf16[512,256]{1,0:T(8,128)(2,1)} %refs_17_.1) | copy-start | bytes 786436
  37.0 1.0 copy-start.1
  37.9 0.6 copy-start.17
  55.2 36.2 %all-to-all-start.3 = ((bf16[32,48,256]{2,1,0:T(8,128)(2,1)}), bf16[32,48,256]{2,1,0:T(8,128)(2,1)}, u32[]{:S(2)}, u32[]{:S(2)}) async-start(bf16[32,48,256]{2,1,0:T(8,128)(2,1)} %copy-done.1), calls=%async_computation.3 | async-start | bytes 1572864 | tf_op jit(solution)/shard_map/all_to_all | solution.py:608
  60.5 2.2 %copy-start.4 = (bf16[8,4,512,128]{3,2,1,0:T(8,128)(2,1)S(1)}, bf16[8,4,512,128]{3,2,1,0:T(8,128)(2,1)}, u32[]{:S(2)}) copy-start(bf16[8,4,512,128]{3,2,1,0:T(8,128)(2,1)} %copy-done.3) | copy-start | bytes 12582916
  62.7 1.6 %copy-start.7 = (s32[8,512,128]{2,1,0:T(8,128)S(1)}, s32[8,512,128]{2,1,0:T(8,128)}, u32[]{:S(2)}) copy-start(s32[8,512,128]{2,1,0:T(8,128)} %copy-done.6) | copy-start | bytes 6291460
  64.3 1.0 copy-start.9
  65.3 0.9 copy-start.13
  66.2 0.9 copy-start.15
  67.1 0.8 copy-start.18
  67.9 0.7 copy-start.21
  68.7 0.7 copy-start.23
  69.3 0.7 copy-start.25
  70.0 0.7 copy-start.28
  70.7 0.7 copy-start.31
  71.3 0.7 copy-start.36
  90.8 0.6 copy-start.33
  92.3 2.2 %copy-start.5 = (bf16[8,4,512,128]{3,2,1,0:T(8,128)(2,1)S(1)}, bf16[8,4,512,128]{3,2,1,0:T(8,128)(2,1)}, u32[]{:S(2)}) copy-start(bf16[8,4,512,128]{3,2,1,0:T(8,128)(2,1)} %copy-done.3) | copy-start | bytes 12582916
  94.5 1.6 %copy-start.8 = (s32[8,512,128]{2,1,0:T(8,128)S(1)}, s32[8,512,128]{2,1,0:T(8,128)}, u32[]{:S(2)}) copy-start(s32[8,512,128]{2,1,0:T(8,128)} %copy-done.6) | copy-start | bytes 6291460
  96.1 1.0 copy-start.10
  97.1 0.9 copy-start.14
  98.0 0.9 copy-start.16
  98.9 0.8 copy-start.19
  99.8 0.7 copy-start.22
  100.5 0.7 copy-start.24
  101.2 0.7 copy-start.26
  101.8 0.7 copy-start.29
  102.5 0.7 copy-start.32
  103.1 0.8 copy-start.34
  104.0 0.7 copy-start.37
